TPU v7x, 32 devices: a whole 2x2x4 slice. The times are simulated.
32 devices in a mesh: dp: 4 (over y, x), ctx: 8 (over z, core).
Axes of the slice: x: 2, y: 2, z: 4, core: 2. Of those that a mesh axis runs over, the one named last changes fastest.
Arguments:
- hidden_in: bfloat16 [4, 3072, 576], P('dp', 'ctx'), may hold values from -6 to 6
- segment_ids: int32 [4, 3072], P('dp', 'ctx'), may hold values from 0 to 3, as said below
- w_query: bfloat16 [576, 576], replicated, may hold values from -0.625 to 0.625
- w_key: bfloat16 [576, 192], replicated, may hold values from -0.25 to 0.25
- w_value: bfloat16 [576, 192], replicated, may hold values from -0.25 to 0.25
- w_out: bfloat16 [576, 576], replicated, may hold values from -0.5 to 0.5
- w_gate: bfloat16 [576, 1536], replicated, may hold values from -0.25 to 0.25
- w_up: bfloat16 [576, 1536], replicated, may hold values from -0.25 to 0.25
- w_down: bfloat16 [1536, 576], replicated, may hold values from -0.15625 to 0.15625
- gain_attn: float32 [576], replicated, may hold values from 0.1 to 1.9
- gain_ffn: float32 [576], replicated, may hold values from 0.1 to 1.9
- out_grad: bfloat16 [4, 3072, 576], P('dp', 'ctx'), may hold values from -6 to 6
Outputs:
- layer_out: bfloat16 [4, 3072, 576], P('dp', 'ctx')
- input_grad: bfloat16 [4, 3072, 576], P('dp', 'ctx')
- grad_query: float32 [576, 576], replicated
- grad_key: float32 [576, 192], replicated
- grad_value: float32 [576, 192], replicated
- grad_out: float32 [576, 576], replicated
- grad_gate: float32 [576, 1536], replicated
- grad_up: float32 [576, 1536], replicated
- grad_down: float32 [1536, 576], replicated
- grad_gain_attn: float32 [576], replicated
- grad_gain_ffn: float32 [576], replicated
Inputs may be any that keep to these rules, and one draw needn't show every extreme that they name: `segment_ids`: ids never fall along a sequence and start at 0; in every sequence one document starts within the first 384 positions and ends within the last 384.
All inputs are finite; a program needn't handle non-finite values.
Results may differ from a plain program's by a relative error of at most 0.02.
Values may be sent and summed in bfloat16 or wider, within the bound.
A program may use at most 128 MiB of HBM per device.

v0:
```python
import math

import jax
import jax.numpy as jnp
from jax import lax
from jax.sharding import PartitionSpec as P

HEADS = 9
KV_HEADS = 3
HEAD_DIM = 64


NORM_EPS = 1e-05
ROPE_BASE = 10000.0
MASKED = -1e30


def shifted(value, axis, steps):
    count = lax.axis_size(axis)
    pairs = [(source, (source + steps) % count) for source in range(count)]
    return lax.ppermute(value, axis, pairs)


def matmul(left_side, right_side):
    return jnp.dot(left_side, right_side, preferred_element_type=jnp.float32)


def times_transposed(left_side, right_side):
    return lax.dot_general(
        left_side, right_side, (((1,), (1,)), ((), ())), preferred_element_type=jnp.float32
    )


def transposed_times(left_side, right_side):
    return lax.dot_general(
        left_side, right_side, (((0,), (0,)), ((), ())), preferred_element_type=jnp.float32
    )


def angles(positions, head_size):
    half_size = head_size // 2
    inverse = ROPE_BASE ** (-jnp.arange(half_size, dtype=jnp.float32) * 2.0 / head_size)
    phase_angle = positions.astype(jnp.float32)[:, None] * inverse[None, :]
    return (jnp.cos(phase_angle)[:, None, :], jnp.sin(phase_angle)[:, None, :])


def rotate(values, cosine, sine_table):
    half_size = values.shape[-1] // 2
    first_half = values[..., :half_size]
    second_half = values[..., half_size:]
    return jnp.concatenate(
        [
            first_half * cosine - second_half * sine_table,
            second_half * cosine + first_half * sine_table,
        ],
        axis=-1,
    )


def unrotate(gradient, cosine, sine_table):
    half_size = gradient.shape[-1] // 2
    first_half = gradient[..., :half_size]
    second_half = gradient[..., half_size:]
    return jnp.concatenate(
        [
            first_half * cosine + second_half * sine_table,
            second_half * cosine - first_half * sine_table,
        ],
        axis=-1,
    )


def norm_forward(values, gain_vector):
    inv_rms = lax.rsqrt(jnp.mean(values * values, axis=-1, keepdims=True) + NORM_EPS)
    unit_rows = values * inv_rms
    return (unit_rows, inv_rms, (unit_rows * gain_vector).astype(jnp.bfloat16))


def norm_backward(gradient, unit_rows, inv_rms, gain_vector):
    gain_grad = jnp.sum(gradient * unit_rows, axis=0)
    inner_grad = gradient * gain_vector
    return (
        inv_rms
        * (inner_grad - unit_rows * jnp.mean(inner_grad * unit_rows, axis=-1, keepdims=True)),
        gain_grad,
    )


def allowed_mask(own_ids, query_index, key_ids, key_index):
    return (own_ids[:, None] == key_ids[None, :]) & (key_index[None, :] <= query_index[:, None])


def on_device(
    hidden_in,
    segment_ids,
    w_query,
    w_key,
    w_value,
    w_out,
    w_gate,
    w_up,
    w_down,
    gain_attn,
    gain_ffn,
    out_grad,
):
    inputs = hidden_in[0].astype(jnp.float32)
    own_ids = segment_ids[0]
    row_count = inputs.shape[0]
    axis_count = lax.axis_size("ctx")
    axis_place = lax.axis_index("ctx")
    groups = HEADS // KV_HEADS
    key_width = KV_HEADS * HEAD_DIM
    score_scale = 1.0 / math.sqrt(HEAD_DIM)
    whole_ids = lax.all_gather(own_ids, "ctx", axis=0, tiled=True)
    query_index = axis_place * row_count + jnp.arange(row_count, dtype=jnp.int32)
    positions = query_index - jnp.searchsorted(whole_ids, own_ids, side="left")
    cosine, sine_table = angles(positions, HEAD_DIM)
    unit_attn, inv_attn, normed = norm_forward(inputs, gain_attn)
    query_rows = rotate(
        matmul(normed, w_query).reshape(row_count, HEADS, HEAD_DIM), cosine, sine_table
    )
    query_rows = query_rows.astype(jnp.bfloat16).reshape(row_count, KV_HEADS, groups, HEAD_DIM)
    key_rows = rotate(
        matmul(normed, w_key).reshape(row_count, KV_HEADS, HEAD_DIM), cosine, sine_table
    )
    key_rows = key_rows.astype(jnp.bfloat16).reshape(row_count, key_width)
    value_rows = matmul(normed, w_value).astype(jnp.bfloat16)
    start_state = (
        jnp.full((KV_HEADS, groups, row_count), MASKED, jnp.float32),
        jnp.zeros((KV_HEADS, groups, row_count), jnp.float32),
        jnp.zeros((KV_HEADS, groups, row_count, HEAD_DIM), jnp.float32),
    )
    carried = start_state
    key_piece = lax.all_gather(key_rows, "ctx", axis=0, tiled=True)
    value_piece = lax.all_gather(value_rows, "ctx", axis=0, tiled=True)
    attend_block_rows = math.gcd(key_piece.shape[0], 512)
    attend_block_count = key_piece.shape[0] // attend_block_rows
    key_blocks = key_piece.reshape(attend_block_count, attend_block_rows, KV_HEADS, HEAD_DIM)
    value_blocks = value_piece.reshape(attend_block_count, attend_block_rows, KV_HEADS, HEAD_DIM)
    offsets = jnp.arange(attend_block_count, dtype=jnp.int32) * attend_block_rows

    def one_block(running, item_in):
        run_max, run_sum, run_acc = running
        key_block, value_block, offset = item_in
        key_index = offset + jnp.arange(attend_block_rows, dtype=jnp.int32)
        key_ids = lax.dynamic_slice_in_dim(whole_ids, offset, attend_block_rows, 0)
        allowed = allowed_mask(own_ids, query_index, key_ids, key_index)
        scores = (
            jnp.einsum("qhgd,khd->hgqk", query_rows, key_block, preferred_element_type=jnp.float32)
            * score_scale
        )
        scores = jnp.where(allowed, scores, MASKED)
        new_max = jnp.maximum(run_max, jnp.max(scores, axis=-1))
        weights = jnp.where(allowed, jnp.exp(scores - new_max[..., None]), 0.0)
        fading = jnp.exp(run_max - new_max)
        run_sum = run_sum * fading + jnp.sum(weights, axis=-1)
        run_acc = run_acc * fading[..., None] + jnp.einsum(
            "hgqk,khd->hgqd",
            weights.astype(jnp.bfloat16),
            value_block,
            preferred_element_type=jnp.float32,
        )
        return ((new_max, run_sum, run_acc), None)

    carried, _ = lax.scan(one_block, carried, (key_blocks, value_blocks, offsets))
    run_max, run_sum, run_acc = carried
    log_sum = run_max + jnp.log(run_sum)
    attended = run_acc / run_sum[..., None]
    attn_mixed = (
        jnp.transpose(attended, (2, 0, 1, 3))
        .reshape(row_count, HEADS * HEAD_DIM)
        .astype(jnp.bfloat16)
    )
    residual = inputs + matmul(attn_mixed, w_out)
    unit_ffn, inv_ffn, normed_ffn = norm_forward(residual, gain_ffn)
    gate_rows = matmul(normed_ffn, w_gate)
    up_proj = matmul(normed_ffn, w_up)
    sigmoid_gate = jax.nn.sigmoid(gate_rows)
    silu_gate = gate_rows * sigmoid_gate
    hidden = (silu_gate * up_proj).astype(jnp.bfloat16)
    layer_out = (residual + matmul(hidden, w_down)).astype(jnp.bfloat16)
    out_cot = out_grad[0]
    grad_down = transposed_times(hidden, out_cot)
    grad_hidden = times_transposed(out_cot, w_down)
    gate_grad = (
        grad_hidden * up_proj * sigmoid_gate * (1.0 + gate_rows * (1.0 - sigmoid_gate))
    ).astype(jnp.bfloat16)
    up_grad = (grad_hidden * silu_gate).astype(jnp.bfloat16)
    grad_gate = transposed_times(normed_ffn, gate_grad)
    grad_up = transposed_times(normed_ffn, up_grad)
    grad_normed_ffn = times_transposed(gate_grad, w_gate) + times_transposed(up_grad, w_up)
    grad_residual, grad_gain_ffn = norm_backward(grad_normed_ffn, unit_ffn, inv_ffn, gain_ffn)
    grad_residual = grad_residual + out_cot.astype(jnp.float32)
    branch_grad = grad_residual.astype(jnp.bfloat16)
    grad_out = transposed_times(attn_mixed, branch_grad)
    mixed_grad = (
        times_transposed(branch_grad, w_out)
        .astype(jnp.bfloat16)
        .reshape(row_count, KV_HEADS, groups, HEAD_DIM)
    )
    delta_rows = jnp.einsum("qhgd,hgqd->hgq", mixed_grad.astype(jnp.float32), attended)
    all_keys, all_values = (
        lax.all_gather(key_rows, "ctx", axis=0, tiled=True),
        lax.all_gather(value_rows, "ctx", axis=0, tiled=True),
    )
    block_rows = math.gcd(row_count, 512)
    block_count = row_count // block_rows
    local_offsets = jnp.arange(block_count, dtype=jnp.int32) * block_rows

    def turn_body(turn_step, carried):
        query_grad, key_grad, value_grad = carried
        owner_place = (axis_place - turn_step) % axis_count
        base_row = owner_place * row_count
        key_span = lax.dynamic_slice_in_dim(all_keys, base_row, row_count, 0).reshape(
            block_count, block_rows, KV_HEADS, HEAD_DIM
        )
        value_span = lax.dynamic_slice_in_dim(all_values, base_row, row_count, 0).reshape(
            block_count, block_rows, KV_HEADS, HEAD_DIM
        )

        def grad_block(query_acc, item_in):
            key_block, value_block, offset = item_in
            key_index = base_row + offset + jnp.arange(block_rows, dtype=jnp.int32)
            key_ids = lax.dynamic_slice_in_dim(whole_ids, base_row + offset, block_rows, 0)
            allowed = allowed_mask(own_ids, query_index, key_ids, key_index)
            scores = (
                jnp.einsum(
                    "qhgd,khd->hgqk", query_rows, key_block, preferred_element_type=jnp.float32
                )
                * score_scale
            )
            prob_rows = jnp.where(allowed, jnp.exp(scores - log_sum[..., None]), 0.0)
            prob_grad = jnp.einsum(
                "qhgd,khd->hgqk", mixed_grad, value_block, preferred_element_type=jnp.float32
            )
            score_grad = (prob_rows * (prob_grad - delta_rows[..., None])).astype(jnp.bfloat16)
            value_part = jnp.einsum(
                "hgqk,qhgd->khd",
                prob_rows.astype(jnp.bfloat16),
                mixed_grad,
                preferred_element_type=jnp.float32,
            )
            key_part = (
                jnp.einsum(
                    "hgqk,qhgd->khd", score_grad, query_rows, preferred_element_type=jnp.float32
                )
                * score_scale
            )
            query_part = (
                jnp.einsum(
                    "hgqk,khd->qhgd", score_grad, key_block, preferred_element_type=jnp.float32
                )
                * score_scale
            )
            return (query_acc + query_part, (key_part, value_part))

        query_grad, (key_parts, value_parts) = lax.scan(
            grad_block, query_grad, (key_span, value_span, local_offsets)
        )
        key_grad = key_grad + key_parts.reshape(row_count, key_width)
        value_grad = value_grad + value_parts.reshape(row_count, key_width)
        key_grad, value_grad = (
            shifted(key_grad.astype(jnp.bfloat16), "ctx", 1).astype(key_grad.dtype),
            shifted(value_grad.astype(jnp.bfloat16), "ctx", 1).astype(value_grad.dtype),
        )
        return (query_grad, key_grad, value_grad)

    start_grads = (
        jnp.zeros((row_count, KV_HEADS, groups, HEAD_DIM), jnp.float32),
        jnp.zeros((row_count, key_width), jnp.float32),
        jnp.zeros((row_count, key_width), jnp.float32),
    )
    query_grad, key_grad, value_grad = lax.fori_loop(0, axis_count, turn_body, start_grads)
    query_back = unrotate(query_grad.reshape(row_count, HEADS, HEAD_DIM), cosine, sine_table)
    query_back = query_back.reshape(row_count, HEADS * HEAD_DIM).astype(jnp.bfloat16)
    key_back = unrotate(key_grad.reshape(row_count, KV_HEADS, HEAD_DIM), cosine, sine_table)
    key_back = key_back.reshape(row_count, key_width).astype(jnp.bfloat16)
    value_back = value_grad.astype(jnp.bfloat16)
    grad_query = transposed_times(normed, query_back)
    grad_key = transposed_times(normed, key_back)
    grad_value = transposed_times(normed, value_back)
    grad_normed = (
        times_transposed(query_back, w_query)
        + times_transposed(key_back, w_key)
        + times_transposed(value_back, w_value)
    )
    grad_inputs, grad_gain_attn = norm_backward(grad_normed, unit_attn, inv_attn, gain_attn)
    input_grad = (grad_residual + grad_inputs).astype(jnp.bfloat16)
    (
        total_query,
        total_key,
        total_value,
        total_out,
        total_gate,
        total_up,
        total_down,
        total_attn,
        total_ffn,
    ) = lax.psum(
        (
            grad_query,
            grad_key,
            grad_value,
            grad_out,
            grad_gate,
            grad_up,
            grad_down,
            grad_gain_attn,
            grad_gain_ffn,
        ),
        ("dp", "ctx"),
    )
    return (
        layer_out[None],
        input_grad[None],
        total_query,
        total_key,
        total_value,
        total_out,
        total_gate,
        total_up,
        total_down,
        total_attn,
        total_ffn,
    )


def solution(mesh):
    return jax.shard_map(
        on_device,
        mesh=mesh,
        in_specs=(
            P("dp", "ctx", None),
            P("dp", "ctx"),
            P(),
            P(),
            P(),
            P(),
            P(),
            P(),
            P(),
            P(),
            P(),
            P("dp", "ctx", None),
        ),
        out_specs=(
            P("dp", "ctx", None),
            P("dp", "ctx", None),
            P(),
            P(),
            P(),
            P(),
            P(),
            P(),
            P(),
            P(),
            P(),
        ),
        check_vma=False,
    )
```

profile of v0, /device:TPU:1, one launch (start us, length us, event | category | flops | bytes accessed | tf_op | source)
XLA Modules:
  0.0 1084.0 jit_solution(11321605811488402078)
XLA Ops:
  8.1 14.4 %all-gather = s32[1,3072]{1,0:T(1,128)S(1)} all-gather(s32[1,384]{1,0:T(1,128)} %param.21), channel_id=2, replica_groups=mesh['dp'=4,'ctx'=8] {'ctx'}, dimensions={1}, use_global_device_ids=true | all-gather | bytes 13824 | tf_op jit(solution)/shard_map/all_gather | solution.py:115
  23.6 31.6 %while.104 = (s32[]{:T(128)}, u32[384]{0:T(512)S(1)}, u32[384]{0:T(512)S(1)}, s32[3072]{0:T(1024)S(1)}, s32[384]{0:T(512)S(1)}, /*index=5*/s32[]{:T(128)}, s32[]{:T(128)}, s32[]{}) while((s32[]{:T(128)}, u32[384]{0:T(512)S(1)}, u32[384]{0:T(512)S(1)}, s32[3072]{0:T(1024)S(1)}, s32[384]{0:T(512)S(1)}, /*index=5*/s32[]{:T(128)}, ...), condition=%wide.region_2.3_spmd.clone, body=%wide.region_1.2_spmd.clone.sunk | while | flops 7940 | bytes 31085 | solution.py:117
  62.2 17.3 %all-gather.4.cloned.1.call-done = bf16[3072,192]{0,1:T(8,128)(2,1)} async-done(((bf16[384,192]{0,1:T(8,128)(2,1)}), bf16[3072,192]{0,1:T(8,128)(2,1)}) %all-gather.4.cloned.1.call-update) | async-done | bytes 1179664 | tf_op jit(solution)/shard_map/all_gather | solution.py:135
  79.6 3.7 reshape.260
  86.1 18.3 %all-gather.6.cloned.1.call-done = bf16[3072,192]{0,1:T(8,128)(2,1)} async-done(((bf16[384,192]{0,1:T(8,128)(2,1)}), bf16[3072,192]{0,1:T(8,128)(2,1)}) %all-gather.6.cloned.1.call-update) | async-done | bytes 1179664 | tf_op jit(solution)/shard_map/all_gather | solution.py:136
  104.4 3.7 reshape.261
  110.9 82.5 %while.105 = (s32[]{:T(128)}, f32[3,3,384]{2,1,0:T(4,128)}, f32[3,3,384]{2,1,0:T(4,128)}, f32[3,3,384,64]{2,3,1,0:T(8,128)S(1)}, s32[1,384]{1,0:T(1,128)}, /*ind...) while((s32[]{:T(128)}, f32[3,3,384]{2,1,0:T(4,128)}, ...), condition=%wide.region_6.7_spmd.clone, body=%wide.region_3.6_spmd.clone.sunk | while | flops 477259520 | bytes 25030700 | solution.py:166
  215.9 574.4 %while.107 = (s32[]{:T(128)}, f32[384,3,3,64]{0,3,2,1:T(8,128)S(1)}, f32[384,192]{0,1:T(8,128)}, f32[384,192]{0,1:T(8,128)}, s32[]{:T(128)}, /*index=5*/bf16[307...) while((s32[]{:T(128)}, f32[384,3,3,64]{0,3,2,1:T(8,128)S(1)}, ...), condition=%wide.region_12.13_spmd.clone, body=%wide.region_9.12_spmd.clone.sunk | while | flops 287416864 | bytes 17744436 | solution.py:274
  224.8 51.7 %while.108 = (s32[]{:T(128)}, f32[384,3,3,64]{0,3,2,1:T(8,128)S(1)}, f32[3,128,3,64]{1,0,3,2:T(4,128)}, f32[3,128,3,64]{1,0,3,2:T(4,128)}, bf16[3,128,3,64]{1,3,...) while((s32[]{:T(128)}, f32[384,3,3,64]{0,3,2,1:T(8,128)S(1)}, ...), condition=%wide.region_11.11_spmd, body=%wide.region_10.10_spmd.sunk | while | flops 286826624 | bytes 12433851 | solution.py:258
  234.5 3.7 dynamic_update_slice.9
  238.3 3.7 dynamic_update_slice.10
  251.8 3.7 dynamic_update_slice.9
  255.5 3.7 dynamic_update_slice.10
  269.0 3.7 dynamic_update_slice.9
  272.8 3.7 dynamic_update_slice.10
  294.2 51.7 %while.108 = (s32[]{:T(128)}, f32[384,3,3,64]{0,3,2,1:T(8,128)S(1)}, f32[3,128,3,64]{1,0,3,2:T(4,128)}, f32[3,128,3,64]{1,0,3,2:T(4,128)}, bf16[3,128,3,64]{1,3,...) while((s32[]{:T(128)}, f32[384,3,3,64]{0,3,2,1:T(8,128)S(1)}, ...), condition=%wide.region_11.11_spmd, body=%wide.region_10.10_spmd.sunk | while | flops 286826624 | bytes 12433851 | solution.py:258
  303.9 3.7 dynamic_update_slice.9
  307.7 3.7 dynamic_update_slice.10
  321.2 3.7 dynamic_update_slice.9
  324.9 3.7 dynamic_update_slice.10
  338.4 3.7 dynamic_update_slice.9
  342.2 3.7 dynamic_update_slice.10
  364.8 51.7 %while.108 = (s32[]{:T(128)}, f32[384,3,3,64]{0,3,2,1:T(8,128)S(1)}, f32[3,128,3,64]{1,0,3,2:T(4,128)}, f32[3,128,3,64]{1,0,3,2:T(4,128)}, bf16[3,128,3,64]{1,3,...) while((s32[]{:T(128)}, f32[384,3,3,64]{0,3,2,1:T(8,128)S(1)}, ...), condition=%wide.region_11.11_spmd, body=%wide.region_10.10_spmd.sunk | while | flops 286826624 | bytes 12433851 | solution.py:258
  374.6 3.7 dynamic_update_slice.9
  378.3 3.7 dynamic_update_slice.10
  391.8 3.7 dynamic_update_slice.9
  395.6 3.7 dynamic_update_slice.10
  409.1 3.7 dynamic_update_slice.9
  412.8 3.7 dynamic_update_slice.10
  436.9 51.7 %while.108 = (s32[]{:T(128)}, f32[384,3,3,64]{0,3,2,1:T(8,128)S(1)}, f32[3,128,3,64]{1,0,3,2:T(4,128)}, f32[3,128,3,64]{1,0,3,2:T(4,128)}, bf16[3,128,3,64]{1,3,...) while((s32[]{:T(128)}, f32[384,3,3,64]{0,3,2,1:T(8,128)S(1)}, ...), condition=%wide.region_11.11_spmd, body=%wide.region_10.10_spmd.sunk | while | flops 286826624 | bytes 12433851 | solution.py:258
  446.7 3.7 dynamic_update_slice.9
  450.4 3.7 dynamic_update_slice.10
  463.9 3.7 dynamic_update_slice.9
  467.7 3.7 dynamic_update_slice.10
  481.2 3.7 dynamic_update_slice.9
  484.9 3.7 dynamic_update_slice.10
  493.2 4.0 collective-permute-done
  509.3 51.7 %while.108 = (s32[]{:T(128)}, f32[384,3,3,64]{0,3,2,1:T(8,128)S(1)}, f32[3,128,3,64]{1,0,3,2:T(4,128)}, f32[3,128,3,64]{1,0,3,2:T(4,128)}, bf16[3,128,3,64]{1,3,...) while((s32[]{:T(128)}, f32[384,3,3,64]{0,3,2,1:T(8,128)S(1)}, ...), condition=%wide.region_11.11_spmd, body=%wide.region_10.10_spmd.sunk | while | flops 286826624 | bytes 12433851 | solution.py:258
  519.1 3.7 dynamic_update_slice.9
  522.9 3.7 dynamic_update_slice.10
  536.4 3.7 dynamic_update_slice.9
  540.1 3.7 dynamic_update_slice.10
  553.6 3.7 dynamic_update_slice.9
  564.6 4.9 collective-permute-done
  581.8 51.7 %while.108 = (s32[]{:T(128)}, f32[384,3,3,64]{0,3,2,1:T(8,128)S(1)}, f32[3,128,3,64]{1,0,3,2:T(4,128)}, f32[3,128,3,64]{1,0,3,2:T(4,128)}, bf16[3,128,3,64]{1,3,...) while((s32[]{:T(128)}, f32[384,3,3,64]{0,3,2,1:T(8,128)S(1)}, ...), condition=%wide.region_11.11_spmd, body=%wide.region_10.10_spmd.sunk | while | flops 286826624 | bytes 12433851 | solution.py:258
  591.5 3.7 dynamic_update_slice.9
  608.8 3.7 dynamic_update_slice.9
  626.0 3.7 dynamic_update_slice.9
  637.1 4.9 collective-permute-done
  654.2 51.7 %while.108 = (s32[]{:T(128)}, f32[384,3,3,64]{0,3,2,1:T(8,128)S(1)}, f32[3,128,3,64]{1,0,3,2:T(4,128)}, f32[3,128,3,64]{1,0,3,2:T(4,128)}, bf16[3,128,3,64]{1,3,...) while((s32[]{:T(128)}, f32[384,3,3,64]{0,3,2,1:T(8,128)S(1)}, ...), condition=%wide.region_11.11_spmd, body=%wide.region_10.10_spmd.sunk | while | flops 286826624 | bytes 12433851 | solution.py:258
  664.0 3.7 dynamic_update_slice.9
  681.2 3.7 dynamic_update_slice.9
  698.5 3.7 dynamic_update_slice.9
  702.2 3.7 dynamic_update_slice.10
  709.5 4.9 collective-permute-done
  726.6 51.7 %while.108 = (s32[]{:T(128)}, f32[384,3,3,64]{0,3,2,1:T(8,128)S(1)}, f32[3,128,3,64]{1,0,3,2:T(4,128)}, f32[3,128,3,64]{1,0,3,2:T(4,128)}, bf16[3,128,3,64]{1,3,...) while((s32[]{:T(128)}, f32[384,3,3,64]{0,3,2,1:T(8,128)S(1)}, ...), condition=%wide.region_11.11_spmd, body=%wide.region_10.10_spmd.sunk | while | flops 286826624 | bytes 12433851 | solution.py:258
  736.4 3.7 dynamic_update_slice.9
  740.1 3.7 dynamic_update_slice.10
  753.7 3.7 dynamic_update_slice.9
  757.4 3.7 dynamic_update_slice.10
  770.9 3.7 dynamic_update_slice.9
  781.9 4.9 collective-permute-done
  803.7 44.8 %all-reduce = (f32[576]{0:T(1024)}, f32[576]{0:T(1024)}) all-reduce(f32[576]{0:T(1024)S(1)} %get-tuple-element.744, f32[576]{0:T(1024)} %get-tuple-element.742), channel_id=1, replica_groups=mesh['dp'=4,'ctx'=8] {'dp','ctx'}, use_global_device_ids=true, to_apply=%region_22.23 | all-reduce | flops 1152 | bytes 9216 | tf_op jit(solution)/shard_map/psum | solution.py:300
  852.7 210.1 %all-reduce.4.cloned.1.call-done = (f32[576,576]{1,0:T(8,128)}, f32[576,192]{0,1:T(8,128)}, f32[576,192]{0,1:T(8,128)}, f32[576,576]{1,0:T(8,128)}, f32[576,1536...) async-done(((f32[576,576]{1,0:T(8,128)}, f32[576,192]{0,1:T(8,128)}, f32[576,192]{0,1:T(8,128)}, f32[576,576]{1,0:T(8,128)}, f32[576,1536]{1,0:T(8,128)}, ...) | async-done | bytes 14155792 | tf_op jit(solution)/shard_map/psum | solution.py:300
  (865 shorter events, 551.1 us)
Async XLA Ops:
  7.2 191.9 %copy-start = (bf16[1536,576]{0,1:T(8,128)(2,1)S(1)}, bf16[1536,576]{0,1:T(8,128)(2,1)}, u32[]{:S(2)}) copy-start(bf16[1536,576]{0,1:T(8,128)(2,1)} %param.28) | copy-start | bytes 5308420
  7.2 72.4 %all-gather.4.cloned.1.call-start = ((), (), s32[]{:S(2)}) async-start(), calls=%async_computation | async-start | bytes 1327104 | tf_op jit(solution)/shard_map/all_gather | solution.py:135
  23.6 36.6 %copy-start.33 = (f32[384]{0:T(512)}, f32[384]{0:T(512)S(1)}, u32[]{:S(2)}) copy-start(f32[384]{0:T(512)S(1)} %add_rsqrt_fusion.1) | copy-start | bytes 4612
  23.6 31.9 %copy-start.1 = (bf16[1,384,576]{1,2,0:T(8,128)(2,1)S(1)}, bf16[1,384,576]{1,2,0:T(8,128)(2,1)}, u32[]{:S(2)}) copy-start(bf16[1,384,576]{1,2,0:T(8,128)(2,1)} %param.20) | copy-start | bytes 1327108
  23.6 31.9 %copy-start.28 = (bf16[576,192]{0,1:T(8,128)(2,1)S(1)}, bf16[576,192]{0,1:T(8,128)(2,1)}, u32[]{:S(2)}) copy-start(bf16[576,192]{0,1:T(8,128)(2,1)} %param.23) | copy-start | bytes 663556
  23.6 31.9 %copy-start.31 = (f32[576]{0:T(1024)S(1)}, f32[576]{0:T(1024)}, u32[]{:S(2)}) copy-start(f32[576]{0:T(1024)} %param.29) | copy-start | bytes 6916
  55.5 6.5 copy-start.19
  55.5 6.5 copy-start.20
  56.7 47.7 %all-gather.6.cloned.1.call-start = ((), (), s32[]{:S(2)}) async-start(), calls=%async_computation.1 | async-start | bytes 1327104 | tf_op jit(solution)/shard_map/all_gather | solution.py:136
  57.9 1005.0 %all-reduce.4.cloned.1.call-start = ((), (), s32[]{:S(2)}) async-start(), calls=%async_computation.2 | async-start | bytes 29097984 | tf_op jit(solution)/shard_map/psum | solution.py:300
  120.9 3.1 copy-start.24
  120.9 3.7 copy-start.42
  134.7 3.7 copy-start.42
  148.5 3.7 copy-start.42
  162.2 3.7 copy-start.42
  176.0 3.7 copy-start.42
  189.7 3.7 copy-start.42
  196.2 9.1 copy-start.7
  233.4 8.6 copy-start.40
  250.7 8.6 copy-start.40
  267.9 8.6 copy-start.40
  278.2 3.6 collective-permute-start
  281.1 2.7 collective-permute-start.1
  302.8 8.6 copy-start.40
  320.1 8.6 copy-start.40
  337.3 8.6 copy-start.40
  347.7 4.9 collective-permute-start
  351.9 2.4 collective-permute-start.1
  373.5 8.6 copy-start.40
  390.7 8.6 copy-start.40
  408.0 8.6 copy-start.40
  418.3 6.4 collective-permute-start
  422.5 3.9 collective-permute-start.1
  445.6 8.6 copy-start.40
  462.8 8.6 copy-start.40
  480.1 8.6 copy-start.40
  490.4 6.7 collective-permute-start
  493.2 5.7 collective-permute-start.1
  518.0 8.6 copy-start.40
  535.3 8.6 copy-start.40
  552.5 8.6 copy-start.40
  562.9 6.7 collective-permute-start
  564.6 6.7 collective-permute-start.1
  590.4 8.6 copy-start.40
  607.7 8.6 copy-start.40
  624.9 8.6 copy-start.40
  635.3 6.7 collective-permute-start
  637.1 6.7 collective-permute-start.1
  662.9 8.6 copy-start.40
  680.1 8.6 copy-start.40
  697.4 8.6 copy-start.40
  707.7 6.7 collective-permute-start
  709.5 6.7 collective-permute-start.1
  735.3 8.6 copy-start.40
  752.5 8.6 copy-start.40
  769.8 8.6 copy-start.40
  780.1 6.7 collective-permute-start
  781.9 6.7 collective-permute-start.1
  790.3 3.3 copy-start.3
  802.1 46.4 %copy-start.5 = (f32[384,576]{0,1:T(8,128)S(1)}, f32[384,576]{0,1:T(8,128)}, u32[]{:S(2)}) copy-start(f32[384,576]{0,1:T(8,128)} %copy-done.4) | copy-start | bytes 2654212
  1062.8 3.5 copy-start.26
  1062.9 4.3 copy-start.18
  1069.1 3.3 copy-start.10
  1072.4 3.3 copy-start.9
  (92 other events, 212.4 us)
Sparse Core Ops, SparseCore 0:
  56.9 22.6 all-gather.3
  81.7 22.6 all-gather.5
  799.6 263.1 all-reduce.3
where the time goes:
time: 1100 us; the launch traced here: 1080 us
  local copies, waits for them, and re-layouts  347 us (32%)
  waiting for transfers between devices  274 us (25%)
  matrix products  207 us (19%)
  other arithmetic  146 us (13%)
  blocking collectives  59.1 us (5%)
  loops' own time  29.9 us (3%)
  between operations  14.2 us (1%)
    psum x1, waiting for transfers between devices, on_device(): lax.psum((grad_query, grad_key, grad_value, grad_out, grad_gate, grad_up,...  210 us
    dynamic_update_slice x48, local copies, waits for them, and re-layouts, turn_body(): lax.scan(grad_block, query_grad, (key_span, value_span, local_offsets))  179 us
    psum x1, blocking collectives, on_device(): lax.psum((grad_query, grad_key, grad_value, grad_out, grad_gate, grad_up,...  44.8 us
    dot_general x24, matrix products, grad_block(): jnp.einsum('qhgd,khd->hgqk', query_rows, key_block, preferred_element_typ...  32.2 us
    gather x12, local copies, waits for them, and re-layouts, on_device(): positions = query_index - jnp.searchsorted(whole_ids, own_ids, side='left')  30.4 us
    dot_general x24, matrix products, grad_block(): jnp.einsum('qhgd,khd->hgqk', mixed_grad, value_block, preferred_element_t...  29.8 us
    ppermute x16, waiting for transfers between devices, shifted(): return lax.ppermute(value, axis, pairs)  28.1 us
    dot_general x24, matrix products, grad_block(): jnp.einsum('hgqk,qhgd->khd', score_grad, query_rows, preferred_element_ty...  26.8 us
  transfers between devices with their start and end apart: 19, of which 19 were waited for; matrix products, arithmetic and copies ran while one was open for 4% of the time, Pallas kernels for 0%

commit v1 on v0

v1 whole, which is shorter than its diff:
```python
import functools
import math

import jax
import jax.numpy as jnp
import numpy as np
from jax import lax
from jax.experimental import pallas as pl
from jax.experimental.pallas import tpu as pltpu
from jax.sharding import PartitionSpec as P

HEADS = 9
KV_HEADS = 3
HEAD_DIM = 64
GROUPS = HEADS // KV_HEADS

NORM_EPS = 1e-05
ROPE_BASE = 10000.0
MASKED = -1e30
LOG2E = 1.4426950408889634
LN2 = 0.6931471805599453
MESH = pl.DeviceIdType.MESH
OUT_ROWS = 640
QUERY_COLUMNS = 256
ID_ROWS = 16
CHUNK = 256
FF_CHUNK = 512
BACK_CHUNK = 384


def matmul(left_side, right_side):
    return jnp.dot(left_side, right_side, preferred_element_type=jnp.float32)


def times_transposed(left_side, right_side):
    return lax.dot_general(
        left_side, right_side, (((1,), (1,)), ((), ())), preferred_element_type=jnp.float32
    )


def transposed_times(left_side, right_side):
    return lax.dot_general(
        left_side, right_side, (((0,), (0,)), ((), ())), preferred_element_type=jnp.float32
    )


def bit_of(place, bit):
    return lax.rem(lax.div(place, bit), 2)


def flipped(axis, bit):
    place = lax.axis_index(axis)
    return {axis: place + (1 - 2 * bit_of(place, bit)) * bit}


def plane_order(dp_count):
    bits = [1 << i for i in range(dp_count.bit_length() - 1)]
    return [("ctx", 1, 1)] + [("dp", bit, bits[(i + 1) % len(bits)]) for i, bit in enumerate(bits)]


def mirrored(size):
    place = lax.axis_index("ctx")
    core, level = lax.rem(place, 2), lax.div(place, 2)
    group = lax.div(level, size) * size
    return {"ctx": 2 * (2 * group + size - 1 - level) + core}


def is_inner(level):
    return lax.rem(level, 2) != lax.rem(lax.div(level, 2), 2)


HALVINGS = 3


def halved_shapes(rows, columns, cuts):
    shapes = []
    for cut in cuts:
        rows, columns = (rows // 2, columns) if cut == "r" else (rows, columns // 2)
        shapes.append((rows, columns))
    return shapes


def landing_shapes(rows, columns, cuts, plane, level_bits):
    shapes = halved_shapes(rows, columns, cuts)
    return shapes + [shapes[-1]] * (plane - len(cuts) + level_bits + 1)


class Summed:
    def __init__(self, order, level_bits, cuts, source, corner, shape, landed, total, send, recv):
        self.order, self.level_bits, self.cuts = order, level_bits, cuts
        self.landed, self.total = landed, total
        self.source, self.corner, self.shape = source, corner, shape
        self.send, self.recv = send, recv
        self.plane = len(order)
        self.count = self.plane + level_bits + 1
        self.final = landed[-1]

    def cut_at(self, corner, shape, cut, pick):
        rows, columns = shape
        row, column = corner
        if cut == "r":
            rows //= 2
            row = row + pick * rows
        else:
            columns //= 2
            column = column + pick * columns
        return (row, column), (rows, columns)

    @staticmethod
    def view(ref, corner, shape):
        row, column = corner
        if not isinstance(row, int):
            row = pl.multiple_of(row, 16)
        if not isinstance(column, int):
            column = pl.multiple_of(column, 128)
        return ref.at[pl.ds(row, shape[0]), pl.ds(column, shape[1])]

    def current(self, stage):
        if stage == 0:
            return self.source, self.corner, self.shape
        return self.landed[stage - 1], (0, 0), self.landed[stage - 1].shape

    def link(self, stage):
        axis, first, second = self.order[stage]
        if first == second:
            return axis, first
        return axis, jnp.where(lax.rem(lax.axis_index("ctx"), 2) == 0, first, second)

    def spot(self, stage):
        axis, bit = self.link(stage)
        return bit_of(lax.axis_index(axis), bit)

    def copy(self, source, target, number, device):
        return pltpu.make_async_remote_copy(
            src_ref=source, dst_ref=target, send_sem=self.send.at[number],
            recv_sem=self.recv.at[number], device_id=device, device_id_type=MESH,
        )

    def outgoing(self, stage):
        ref, corner, shape = self.current(stage)
        if stage < self.plane:
            device = flipped(*self.link(stage))
            if stage < len(self.cuts):
                corner, shape = self.cut_at(corner, shape, self.cuts[stage], 1 - self.spot(stage))
        elif stage == self.plane or stage == self.count - 1:
            device = mirrored(2)
        else:
            device = mirrored(2 << (stage - self.plane))
        source = self.final if stage == self.count - 1 else self.view(ref, corner, shape)
        return self.copy(source, self.landed[stage], stage, device)

    def add(self, stage, target=None):
        ref, corner, shape = self.current(stage)
        if stage < len(self.cuts):
            corner, shape = self.cut_at(corner, shape, self.cuts[stage], self.spot(stage))
        landed = self.landed[stage]
        target = landed if target is None else target
        row, column = corner
        if not isinstance(column, int):
            column = pl.multiple_of(column, 128)
        take = next(rows for rows in (80, 48, 64, 32, 16) if shape[0] % rows == 0)

        def some(step, carry):
            at = step * take
            near = ref[pl.ds(pl.multiple_of(row + at, 16), take), pl.ds(column, shape[1])]
            here = pl.ds(pl.multiple_of(at, 16), take)
            both = near.astype(jnp.float32) + landed[here, :].astype(jnp.float32)
            target[here, :] = both.astype(jnp.bfloat16)
            return carry

        lax.fori_loop(0, shape[0] // take, some, 0)

    def share(self, depth):
        corner, shape = (0, 0), self.shape
        for stage in range(depth):
            corner, shape = self.cut_at(corner, shape, self.cuts[stage], self.spot(stage))
        return self.view(self.total, (corner[0] + self.corner[0], corner[1] + self.corner[1]), shape)

    def settle(self):
        return pltpu.make_async_copy(
            self.final, self.share(len(self.cuts)), self.send.at[self.count + len(self.cuts)]
        )

    def handing(self, back):
        stage = len(self.cuts) - 1 - back
        mine = self.share(stage + 1)
        return self.copy(
            self.final if back == 0 else mine, mine, self.count + back, flipped(*self.link(stage))
        )

    def run(self, op, inner):
        if op == 0:
            self.outgoing(0).start()
        elif op <= self.plane:
            self.outgoing(op - 1).wait_recv()
            self.add(op - 1)
            if op < self.plane:
                self.outgoing(op).start()
            else:
                @pl.when(jnp.logical_not(inner))
                def _():
                    self.outgoing(op).start()
        elif op < self.count:
            @pl.when(inner)
            def _():
                self.outgoing(op - 1).wait_recv()
                if op < self.count - 1:
                    self.add(op - 1)
                else:
                    self.add(op - 1, self.final)
                self.outgoing(op).start()
                if op == self.count - 1:
                    self.handing(0).start()
                    self.settle().start()
        elif op == self.count:
            @pl.when(jnp.logical_not(inner))
            def _():
                self.outgoing(op - 1).wait_recv()
                self.handing(0).start()
                self.settle().start()
        else:
            back = op - self.count - 1
            self.handing(back).wait_recv()
            if back == 0:
                self.settle().wait()
            if back + 1 < len(self.cuts):
                self.handing(back + 1).start()

    def drain(self, inner):
        for stage in range(self.plane):
            self.outgoing(stage).wait_send()

        @pl.when(inner)
        def _():
            for stage in range(self.plane + 1, self.count):
                self.outgoing(stage).wait_send()

        @pl.when(jnp.logical_not(inner))
        def _():
            self.outgoing(self.plane).wait_send()

        for back in range(len(self.cuts)):
            self.handing(back).wait_send()


RATES = {"core": 250e3, "dp": 85e3, "ctx": 42e3}
HOP_US = 2.0
STEP_US = 1.15
FEED_US = 3.0
OUT_US = 3.0
TAIL_US = 2.0


def planned(jobs, slots, relayed):
    work = []
    for plane, level_bits, cuts, size, _ in jobs:
        sizes = []
        for stage in range(plane):
            size = size / 2 if stage < len(cuts) else size
            sizes.append(("dp" if stage else "core", size))
        levels = [("ctx", size)] * (level_bits + 1)
        levels = [(name + str(number), size) for number, (name, size) in enumerate(levels)]
        work.append(sizes + levels + sizes[: len(cuts)][::-1])
    free, arrival, done, plan = {}, {}, [0] * len(jobs), []

    def issue(number, now):
        stage = done[number]
        if stage < len(work[number]):
            link, size = work[number][stage]
            free[link] = max(now, free.get(link, 0.0)) + size / RATES[link.rstrip("0123456789")]
            arrival[number] = free[link] + HOP_US
        done[number] += 1

    def live():
        return [n for n in range(len(jobs)) if 0 < done[n] <= len(work[n])]

    now = 0.0
    for slot, end in enumerate(slots):
        now = max(now, end)
        if slot in relayed:
            for link in ("ctx0", "ctx1"):
                free[link] = max(free.get(link, 0.0), now) + 2.2
        for number, job in enumerate(jobs):
            if job[4] == slot:
                plan.append((slot, number, 0))
                issue(number, now)
        for number in sorted((n for n in live() if arrival[n] <= now), key=lambda n: -done[n]):
            plan.append((slot, number, done[number]))
            now += 0.2
            issue(number, now)
    while live():
        number = min(live(), key=lambda n: (max(arrival[n] - now, 0.0), -done[n]))
        now = max(now, arrival[number]) + 0.2
        plan.append((len(slots), number, done[number]))
        issue(number, now)
    return plan


def greet(certain, perhaps):
    barrier = pltpu.get_barrier_semaphore()
    for target in certain:
        pl.semaphore_signal(barrier, inc=1, device_id=target, device_id_type=MESH)
    for target, there in perhaps:
        @pl.when(there)
        def _(target=target):
            pl.semaphore_signal(barrier, inc=1, device_id=target, device_id_type=MESH)


def await_peers(certain, perhaps):
    count = len(certain)
    for _, there in perhaps:
        count = count + there.astype(jnp.int32)
    pl.semaphore_wait(pltpu.get_barrier_semaphore(), count)


def before(ids, id_row):
    ids = ids[:1].astype(jnp.float32)
    first = jnp.zeros(id_row.shape, jnp.float32)
    for value in range(3):
        number = jnp.sum((ids == value).astype(jnp.float32), axis=1, keepdims=True)
        first += jnp.where(id_row > value, number, 0.0)
    return first.astype(jnp.int32)


def first_allowed(kv_ref, chip, id_row):
    return before(kv_ref[chip, pl.ds(0, ID_ROWS), :], id_row)


def first_in_half(kv_ref, chip, columns, id_row):
    return before(kv_ref[chip, pl.ds(0, ID_ROWS), columns], id_row)


def turn(values, cosine, sine_table):
    half_size = HEAD_DIM // 2
    first_half = values[:half_size]
    second_half = values[half_size:]
    return jnp.concatenate(
        [
            first_half * cosine - second_half * sine_table,
            second_half * cosine + first_half * sine_table,
        ],
        axis=0,
    )


def as_column(row):
    return jnp.broadcast_to(row, (8, row.shape[1])).T[:, :1]


def layer_kernel(
    order, level_bits, jobs, pumps, after,
    x_ref, id_ref, attn_gain_ref, ffn_gain_ref, cosine_in, sine_in, inverse_in,
    query_hbm, key_hbm, value_hbm, out_hbm, gate_hbm, up_hbm, down_hbm, cotangent_hbm,
    layer_out, input_grad, down_total, gate_total, up_total, out_total, query_total,
    kv_total,
    query_w, key_w, value_w, out_w, gate_w, up_w, down_w, cotangent_ref,
    kv, query_ref, query_pad, grad_ref, grad_pad, first_ref, normed_t, attended, acc, top,
    delta_ref, mixed_t, residual_t, unit_t, normed_grad, back, part, from_mate, from_above, turned_kv,
    turned_query, back_cosine, back_sine, turned_cotangent,
    down_part, gate_part, up_part, out_part, query_part, kv_part, lands,
    loads, up_send, below_recv, over_send, over_recv, mate_send, mate_recv, down_send, above_recv,
    sum_send, sum_recv,
):
    place = lax.axis_index("ctx")
    core, level = lax.rem(place, 2), lax.div(place, 2)
    levels, _, span = kv.shape
    rows = span // 2
    features = x_ref.shape[0]
    wide = gate_w.shape[1]
    count = KV_HEADS * levels
    mate = {"ctx": place + 1 - 2 * core}
    below = {"ctx": place - 2}
    above = {"ctx": place + 2}
    own = pl.ds(pl.multiple_of(core * rows, 128), rows)

    weights = [
        pltpu.make_async_copy(source, target, loads.at[number])
        for number, (source, target) in enumerate(
            (
                (key_hbm, key_w), (value_hbm, value_w), (query_hbm, query_w), (out_hbm, out_w),
                (gate_hbm, gate_w), (up_hbm, up_w), (down_hbm, down_w),
                (cotangent_hbm, cotangent_ref),
            )
        )
    ]
    for copy in weights:
        copy.start()

    carries = is_inner(level)
    side = 2 * bit_of(level, 1) - 1
    other = level + side
    certain = [flipped(axis, bit) for axis, bit, _ in order] + [mirrored(2)]
    perhaps = [({"ctx": place + 2 * side}, (other >= 0) & (other < levels))]
    perhaps += [(mirrored(2 << bit), carries) for bit in range(2, level_bits)]
    greet(certain, perhaps)

    sources = [(down_part, down_total), (gate_part, gate_total), (up_part, up_total)]
    places = [(*pair, (0, at)) for at in range(0, wide, FF_CHUNK) for pair in sources]
    places += [(out_part, out_total, (0, 0))]
    for head in range(KV_HEADS):
        places += [
            (query_part, query_total, (head * features, 0)),
            (kv_part, kv_total, (head * 2 * HEAD_DIM, 0)),
        ]
    streams = [
        Summed(
            order, level_bits, cuts, source, corner, shape, lands[number], total,
            sum_send.at[number], sum_recv.at[number],
        )
        for number, ((source, total, corner), (cuts, shape)) in enumerate(zip(places, jobs))
    ]

    def pump(slot):
        for number, op in pumps.get(slot, ()):
            streams[number].run(op, carries)

    x = x_ref[...].astype(jnp.float32)
    mean = jnp.sum(x * x, axis=0, keepdims=True) * (1.0 / features)
    inverse_attn = lax.rsqrt(mean + NORM_EPS)
    attn_gain = as_column(attn_gain_ref[...].reshape(1, features))
    normed_t[...] = (x * inverse_attn * attn_gain).astype(jnp.bfloat16)
    base = (place * rows).astype(jnp.float32) * inverse_in[...]
    base_cosine, base_sine = jnp.cos(base), jnp.sin(base)
    cosine = base_cosine * cosine_in[...] - base_sine * sine_in[...]
    sine_table = base_sine * cosine_in[...] + base_cosine * sine_in[...]
    kv[level, pl.ds(0, ID_ROWS), own] = jnp.broadcast_to(
        id_ref[...].astype(jnp.float32), (ID_ROWS, rows)
    ).astype(jnp.bfloat16)
    weights[0].wait()
    weights[1].wait()

    def piece_rows(head):
        if head == 0:
            return pl.ds(0, ID_ROWS + 2 * HEAD_DIM)
        return pl.ds(ID_ROWS + 2 * HEAD_DIM * head, 2 * HEAD_DIM)

    def upward(chip, head):
        return pltpu.make_async_remote_copy(
            src_ref=kv.at[chip, piece_rows(head), own], dst_ref=kv.at[chip, piece_rows(head), own],
            send_sem=up_send.at[chip, head], recv_sem=below_recv.at[chip, head],
            device_id=above, device_id_type=MESH,
        )

    def across(chip, head):
        return pltpu.make_async_remote_copy(
            src_ref=kv.at[chip, piece_rows(head), own], dst_ref=kv.at[chip, piece_rows(head), own],
            send_sem=over_send.at[chip, head], recv_sem=over_recv.at[chip, head],
            device_id=mate, device_id_type=MESH,
        )

    def hand_on(chip, head):
        @pl.when(level < levels - 1)
        def _():
            upward(chip, head).start()

        across(chip, head).start()

    keys = matmul(key_w[...], normed_t[...])
    values = matmul(value_w[...], normed_t[...])
    await_peers(certain, perhaps)
    for head in range(KV_HEADS):
        at = head * HEAD_DIM
        key = turn(keys[at : at + HEAD_DIM], cosine, sine_table)
        both = jnp.concatenate([key, values[at : at + HEAD_DIM]], axis=0)
        kv[level, pl.ds(ID_ROWS + 2 * at, 2 * HEAD_DIM), own] = both.astype(jnp.bfloat16)
        hand_on(level, head)
    weights[2].wait()
    queries = transposed_times(query_w[...], normed_t[...])
    scale = LOG2E / math.sqrt(HEAD_DIM)
    for head in range(KV_HEADS):
        for group in range(GROUPS):
            at = (head * GROUPS + group) * HEAD_DIM
            query = turn(queries[at : at + HEAD_DIM], cosine, sine_table) * scale
            query_ref[head, :, group * rows : (group + 1) * rows] = query.astype(jnp.bfloat16)
    nothing = jnp.zeros((HEAD_DIM, rows), jnp.bfloat16)
    for head in range(KV_HEADS):
        for group in range(GROUPS):
            piece = slice(group * rows, (group + 1) * rows)
            query_pad[head, piece, :] = jnp.concatenate(
                [query_ref[head, :, piece], nothing], axis=0
            ).T
    weights[7].wait()
    turned_cotangent[...] = cotangent_ref[...].T
    acc[...] = jnp.zeros_like(acc)
    top[...] = jnp.full_like(top, MASKED)
    id_row = jnp.concatenate([id_ref[...].astype(jnp.float32)] * GROUPS, axis=1)
    local = jnp.concatenate([lax.broadcasted_iota(jnp.int32, (1, rows), 1)] * GROUPS, axis=1)
    index = place * rows + local
    ones = jnp.ones((16, rows), jnp.bfloat16)

    def attend_block(chip, half, careful):
        begin = half * rows
        columns = pl.ds(pl.multiple_of(begin, 128), rows)
        first = first_ref[chip] - begin
        limit = index - chip * span - begin
        inside = first <= 0
        for head in range(KV_HEADS):
            key_at = ID_ROWS + 2 * HEAD_DIM * head
            key_t = kv[chip, pl.ds(key_at, HEAD_DIM), columns]
            value_t = kv[chip, pl.ds(key_at + HEAD_DIM, HEAD_DIM), columns]
            scores = transposed_times(key_t, query_ref[head])
            old = top[head]
            if careful:
                key_index = lax.broadcasted_iota(jnp.int32, scores.shape, 0)
                allowed = (key_index >= first) & (key_index <= limit)
                scores = jnp.where(allowed, scores, 2 * MASKED)
            new = jnp.maximum(old, jnp.max(scores, axis=0, keepdims=True))
            less = new
            if not careful:
                new = jnp.where(inside, new, old)
                less = jnp.where(inside, new, -MASKED)
            probs = jnp.exp2(scores - less).astype(jnp.bfloat16)
            acc[head] = acc[head] * jnp.exp2(old - new) + matmul(
                jnp.concatenate([value_t, ones], axis=0), probs
            )
            top[head] = new

    def one_block(turn_number, carry):
        chip, mates = level - lax.div(turn_number, 2), lax.rem(turn_number, 2)
        half = core + mates * (1 - 2 * core)
        block = 2 * chip + half

        @pl.when(chip >= 0)
        def _():
            for head in range(KV_HEADS):
                @pl.when((mates == 0) & (chip < level))
                def _(head=head):
                    upward(chip, head).wait_recv()
                    hand_on(chip, head)

                @pl.when(mates == 1)
                def _(head=head):
                    across(chip, head).wait_recv()

            @pl.when(mates == 1)
            def _():
                first_ref[chip] = first_allowed(kv, chip, id_row)

            @pl.when(mates == 0)
            def _():
                first_ref[chip] = first_in_half(kv, chip, own, id_row) + half * rows

            edge = (block == 0) | (block == place)

            @pl.when((block <= place) & edge)
            def _():
                attend_block(chip, half, True)

            @pl.when((block < place) & jnp.logical_not(edge))
            def _():
                attend_block(chip, half, False)

        return carry

    lax.fori_loop(0, 2 * levels, one_block, 0)
    for head in range(KV_HEADS):
        total = acc[head, HEAD_DIM : HEAD_DIM + 1, :]
        result = acc[head, :HEAD_DIM, :] * (1.0 / total)
        attended[head] = result
        top[head] = top[head] + jnp.log2(total)
        for group in range(GROUPS):
            at = (head * GROUPS + group) * HEAD_DIM
            piece = result[:, group * rows : (group + 1) * rows]
            mixed_t[pl.ds(at, HEAD_DIM), :] = piece.astype(jnp.bfloat16)

    for copy in weights[3:7]:
        copy.wait()
    residual = x_ref[...].astype(jnp.float32) + transposed_times(out_w[...], mixed_t[...])
    mean = jnp.sum(residual * residual, axis=0, keepdims=True) * (1.0 / features)
    inverse_ffn = lax.rsqrt(mean + NORM_EPS)
    ffn_gain = as_column(ffn_gain_ref[...].reshape(1, features))
    normed_ffn_t = (residual * inverse_ffn * ffn_gain).astype(jnp.bfloat16)
    normed_ffn = normed_ffn_t.T
    cotangent_t = cotangent_ref[...]
    cotangent = turned_cotangent[...]
    residual_t[...] = residual
    unit_t[...] = residual * inverse_ffn
    normed_grad[...] = jnp.zeros_like(normed_grad)
    for number, at in enumerate(range(0, wide, FF_CHUNK)):
        piece = slice(at, at + FF_CHUNK)
        gate = matmul(normed_ffn, gate_w[:, piece])
        up = matmul(normed_ffn, up_w[:, piece])
        sigmoid = 1.0 / (1.0 + jnp.exp(-gate))
        silu = gate * sigmoid
        hidden = (silu * up).astype(jnp.bfloat16)
        down_part[:, piece] = matmul(cotangent_t, hidden).astype(jnp.bfloat16)
        streams[3 * number].run(0, carries)
        grad_hidden = matmul(cotangent, down_w[:, piece])
        gate_grad = (grad_hidden * up * sigmoid * (1.0 + gate * (1.0 - sigmoid))).astype(
            jnp.bfloat16
        )
        up_grad = (grad_hidden * silu).astype(jnp.bfloat16)
        gate_part[:, piece] = matmul(normed_ffn_t, gate_grad).astype(jnp.bfloat16)
        streams[3 * number + 1].run(0, carries)
        up_part[:, piece] = matmul(normed_ffn_t, up_grad).astype(jnp.bfloat16)
        streams[3 * number + 2].run(0, carries)
        residual_t[...] += times_transposed(down_w[:, piece], hidden)
        normed_grad[...] += times_transposed(gate_w[:, piece], gate_grad) + times_transposed(
            up_w[:, piece], up_grad
        )
        pump(number)
    layer_out[...] = residual_t[...].astype(jnp.bfloat16)
    unit = unit_t[...]
    grad_normed = normed_grad[...]
    gain_grad = jnp.sum(grad_normed * unit, axis=1, keepdims=True)
    inner = grad_normed * ffn_gain
    mean = jnp.sum(inner * unit, axis=0, keepdims=True) * (1.0 / features)
    branch = cotangent_t.astype(jnp.float32) + inverse_ffn * (inner - unit * mean)
    residual_t[...] = branch
    branch = branch.astype(jnp.bfloat16)
    out_grads = times_transposed(mixed_t[...], branch)
    fill = jnp.broadcast_to(gain_grad, (features, out_part.shape[0] - features)).T
    out_part[:features, :] = out_grads.astype(jnp.bfloat16)
    out_part[features:, :] = fill.astype(jnp.bfloat16)
    chunks = wide // FF_CHUNK
    streams[3 * chunks].run(0, carries)
    mixed_grad = matmul(out_w[...], branch).astype(jnp.bfloat16)
    for head in range(KV_HEADS):
        for group in range(GROUPS):
            at = (head * GROUPS + group) * HEAD_DIM
            piece = slice(group * rows, (group + 1) * rows)
            grad = mixed_grad[at : at + HEAD_DIM, :]
            grad_ref[head, :, piece] = grad
            delta_ref[head, :, piece] = jnp.sum(
                grad.astype(jnp.float32) * attended[head, :, piece], axis=0, keepdims=True
            )
            grad_pad[head, piece, :] = jnp.concatenate([nothing, grad], axis=0).T
    pump(chunks)
    back[...] = jnp.zeros_like(back)

    def attend_back(step, half, careful):
        head = lax.div(step, levels)
        chip = lax.rem(step, levels)
        key_at = pl.multiple_of(ID_ROWS + 2 * HEAD_DIM * head, 16)
        value_at = pl.multiple_of(ID_ROWS + 2 * HEAD_DIM * head + HEAD_DIM, 16)
        begin = half * rows
        first = first_ref[chip] - begin
        limit = index - chip * span - begin
        less = top[head]
        if not careful:
            less = jnp.where(first <= 0, less, -MASKED)
        for at in range(0, rows, BACK_CHUNK):
            size = min(BACK_CHUNK, rows - at)
            columns = pl.ds(pl.multiple_of(begin + at, 128), size)
            key_t = kv[chip, pl.ds(key_at, HEAD_DIM), columns]
            value_t = kv[chip, pl.ds(value_at, HEAD_DIM), columns]
            scores = transposed_times(key_t, query_ref[head])
            if careful:
                key_index = at + lax.broadcasted_iota(jnp.int32, scores.shape, 0)
                allowed = (key_index >= first) & (key_index <= limit)
                scores = jnp.where(allowed, scores, MASKED)
            probs = jnp.exp2(scores - less)
            prob_grad = transposed_times(value_t, grad_ref[head])
            score_grad = (probs * (prob_grad - delta_ref[head])).astype(jnp.bfloat16)
            kv_back = matmul(score_grad, query_pad[head]) + matmul(
                probs.astype(jnp.bfloat16), grad_pad[head]
            )
            part[step, pl.ds(pl.multiple_of(begin + at, 128), size), :] = kv_back.astype(
                jnp.bfloat16
            )
            back[head] += matmul(key_t, score_grad)

    mate_rows = pl.ds(pl.multiple_of((1 - core) * rows, 128), rows)

    def to_mate(step):
        return pltpu.make_async_remote_copy(
            src_ref=part.at[step, mate_rows], dst_ref=from_mate.at[step],
            send_sem=mate_send.at[step], recv_sem=mate_recv.at[step],
            device_id=mate, device_id_type=MESH,
        )

    def to_below(step):
        return pltpu.make_async_remote_copy(
            src_ref=part.at[step, own], dst_ref=from_above.at[step],
            send_sem=down_send.at[step], recv_sem=above_recv.at[step],
            device_id=below, device_id_type=MESH,
        )

    def collect(step):
        chip = lax.rem(step, levels)
        to_mate(step).wait_recv()
        both = part[step, own, :].astype(jnp.float32) + from_mate[step].astype(jnp.float32)
        part[step, own, :] = both.astype(jnp.bfloat16)

        @pl.when(level < levels - 1)
        def _():
            to_below(step).wait_recv()
            more = part[step, own, :].astype(jnp.float32) + from_above[step].astype(jnp.float32)
            part[step, own, :] = more.astype(jnp.bfloat16)

        @pl.when(chip < level)
        def _():
            to_below(step).start()

    base = (place * rows).astype(jnp.float32) * inverse_in[...]
    base_cosine, base_sine = jnp.cos(base), -jnp.sin(base)
    back_cosine[...] = base_cosine * cosine_in[...] + base_sine * sine_in[...]
    back_sine[...] = base_sine * cosine_in[...] - base_cosine * sine_in[...]

    def head_done(head):
        cosine, sine_table = back_cosine[...], back_sine[...]
        step = head * levels + level
        both = part[step, own, :].astype(jnp.float32).T
        key_back = turn(both[:HEAD_DIM] * LN2, cosine, sine_table).astype(jnp.bfloat16)
        value_back = both[HEAD_DIM:].astype(jnp.bfloat16)
        kv_back = jnp.concatenate([key_back, value_back], axis=0)
        at = pl.multiple_of(head * 2 * HEAD_DIM, 2 * HEAD_DIM)
        turned_kv[pl.ds(at, 2 * HEAD_DIM), :] = kv_back
        kv_part[pl.ds(at, 2 * HEAD_DIM), :] = times_transposed(kv_back, normed_t[...]).astype(
            jnp.bfloat16
        )
        query_back = jnp.concatenate(
            [
                turn(
                    back[head, :, group * rows : (group + 1) * rows] * (1.0 / math.sqrt(HEAD_DIM)),
                    cosine, sine_table,
                ).astype(jnp.bfloat16)
                for group in range(GROUPS)
            ],
            axis=0,
        )
        wide_at = pl.multiple_of(head * GROUPS * HEAD_DIM, HEAD_DIM)
        turned_query[pl.ds(wide_at, GROUPS * HEAD_DIM), :] = query_back
        spare = jnp.zeros((features, QUERY_COLUMNS - GROUPS * HEAD_DIM), jnp.float32)
        query_part[pl.ds(pl.multiple_of(head * features, features), features), :] = jnp.concatenate(
            [times_transposed(normed_t[...], query_back), spare], axis=1
        ).astype(jnp.bfloat16)

    def one_step(turn_number, carry):
        step, own_turn = lax.div(turn_number, 2), lax.rem(turn_number, 2)
        half = core + (1 - own_turn) * (1 - 2 * core)
        chip = lax.rem(step, levels)
        block = 2 * chip + half

        @pl.when((step < count) & (chip <= level))
        def _():
            edge = (block == 0) | (block == place)

            @pl.when((block <= place) & edge)
            def _():
                attend_back(step, half, True)

            @pl.when((block < place) & jnp.logical_not(edge))
            def _():
                attend_back(step, half, False)

            @pl.when(block > place)
            def _():
                part[step, mate_rows, :] = jnp.zeros((rows, 2 * HEAD_DIM), jnp.bfloat16)

            @pl.when(own_turn == 0)
            def _():
                to_mate(step).start()

        due = step - levels + level

        @pl.when((own_turn == 1) & (due >= 0) & (due < count))
        def _():
            @pl.when(lax.rem(due, levels) <= level)
            def _():
                collect(due)

        ended = lax.div(step, levels) - 1

        @pl.when((own_turn == 1) & (step > 0) & (lax.rem(step, levels) == 0))
        def _():
            head_done(ended)
            for head in range(KV_HEADS):
                @pl.when(ended == head)
                def _(head=head):
                    if head < KV_HEADS - 1:
                        streams[3 * chunks + 1 + 2 * head].run(0, carries)
                    streams[3 * chunks + 2 + 2 * head].run(0, carries)

        for slot in sorted(pumps):
            if slot > chunks:
                @pl.when(turn_number == slot - chunks - 1)
                def _(slot=slot):
                    pump(slot)

        return carry

    lax.fori_loop(0, 2 * (count + 1), one_step, 0)

    grad_t = matmul(query_w[...], turned_query[...])
    for head in range(KV_HEADS):
        at = head * HEAD_DIM
        weight = jnp.concatenate(
            [key_w[at : at + HEAD_DIM, :], value_w[at : at + HEAD_DIM, :]], axis=0
        )
        grad_t += transposed_times(weight, turned_kv[2 * at : 2 * at + 2 * HEAD_DIM, :])
    x = x_ref[...].astype(jnp.float32)
    mean = jnp.sum(x * x, axis=0, keepdims=True) * (1.0 / features)
    inverse_attn = lax.rsqrt(mean + NORM_EPS)
    unit = x * inverse_attn
    gain_column = jnp.sum(grad_t * unit, axis=1, keepdims=True)
    last_rows = slice((KV_HEADS - 1) * features, KV_HEADS * features)
    last = query_part[last_rows, QUERY_COLUMNS - 128 :].astype(jnp.float32)
    spare = lax.broadcasted_iota(jnp.int32, last.shape, 1) >= HEAD_DIM
    query_part[last_rows, QUERY_COLUMNS - 128 :] = jnp.where(spare, gain_column, last).astype(
        jnp.bfloat16
    )
    streams[3 * chunks + 2 * KV_HEADS - 1].run(0, carries)
    inner = grad_t * as_column(attn_gain_ref[...].reshape(1, features))
    mean = jnp.sum(inner * unit, axis=0, keepdims=True) * (1.0 / features)
    input_grad[...] = (residual_t[...] + inverse_attn * (inner - unit * mean)).astype(jnp.bfloat16)
    for number, op in after:
        streams[number].run(op, carries)
    for stream in streams:
        stream.drain(carries)

    def ended(step, carry):
        chip = lax.rem(step, levels)

        @pl.when(chip <= level)
        def _():
            to_mate(step).wait_send()

        @pl.when(chip < level)
        def _():
            to_below(step).wait_send()

        return carry

    lax.fori_loop(0, count, ended, 0)

    def handed_on(chip, carry):
        @pl.when(chip <= level)
        def _():
            for head in range(KV_HEADS):
                across(chip, head).wait_send()

                @pl.when(level < levels - 1)
                def _(head=head):
                    upward(chip, head).wait_send()

        return carry

    lax.fori_loop(0, levels, handed_on, 0)


def rotary_tables(rows):
    half_size = HEAD_DIM // 2
    inverse = (ROPE_BASE ** (-np.arange(half_size, dtype=np.float64) * 2.0 / HEAD_DIM))[:, None]
    phase = inverse * np.arange(rows, dtype=np.float64)[None, :]
    return tuple(
        jnp.asarray(table, jnp.float32) for table in (np.cos(phase), np.sin(phase), inverse)
    )


def layer(x_t, ids, attn_gain, ffn_gain, w_query, w_key_t, w_value_t, w_out, w_gate, w_up,
          w_down_t, cotangent_t):
    dp_count, ctx_count = lax.axis_size("dp"), lax.axis_size("ctx")
    order = plane_order(dp_count)
    level_bits = (ctx_count // 2).bit_length() - 1
    levels = ctx_count // 2
    features, rows = x_t.shape
    wide = w_gate.shape[1]
    span, queries = 2 * rows, GROUPS * rows
    count = KV_HEADS * levels
    chunks = wide // FF_CHUNK

    heads = [("rrc", (features, QUERY_COLUMNS)), ("rrr", (2 * HEAD_DIM, features))] * KV_HEADS
    jobs = [("rrc", (features, FF_CHUNK))] * (3 * chunks) + [("rrr", (OUT_ROWS, features))] + heads
    slots = [FEED_US * number for number in range(chunks)]
    slots.append(slots[-1] + OUT_US)
    turns = 2 * (count + 1)
    slots += [slots[-1] + STEP_US * (number + 1) for number in range(turns)]
    slots.append(slots[-1] + TAIL_US)
    begins = [number // 3 for number in range(3 * chunks)] + [chunks]
    for head in range(KV_HEADS):
        begins += [chunks + 2 * (head + 1) * levels + 2] * 2
    begins[-2] = len(slots) - 1
    relayed = [
        chunks + 2 + 2 * step for step in range(count) if step % levels < levels - 1
    ]
    pumps, after = {}, []
    for slot, number, op in planned(
        [
            (len(order), level_bits, cuts, 2 * shape[0] * shape[1], begin)
            for (cuts, shape), begin in zip(jobs, begins)
        ],
        slots, relayed,
    ):
        if op == 0:
            continue
        if slot <= chunks + turns:
            pumps.setdefault(slot, []).append((number, op))
        else:
            after.append((number, op))

    vmem = lambda shape, dtype=jnp.bfloat16: pltpu.VMEM(shape, dtype)
    lands = [
        [vmem(size) for size in landing_shapes(*shape, cuts, len(order), level_bits)]
        for cuts, shape in jobs
    ]
    dma = lambda *shape: pltpu.SemaphoreType.DMA(shape)
    semaphores = len(order) + level_bits + HALVINGS + 2
    head_t = (KV_HEADS, HEAD_DIM, queries)
    padded = (KV_HEADS, queries, 2 * HEAD_DIM)
    row = (KV_HEADS, 1, queries)
    f32 = jnp.float32
    totals = [(features, wide)] * 3 + [(OUT_ROWS, features)]
    totals += [(KV_HEADS * features, QUERY_COLUMNS), (2 * KV_HEADS * HEAD_DIM, features)]
    anywhere = pl.BlockSpec(memory_space=pl.ANY)
    return pl.pallas_call(
        functools.partial(layer_kernel, order, level_bits, jobs, pumps, after),
        out_shape=tuple(
            jax.ShapeDtypeStruct(shape, jnp.bfloat16) for shape in [(features, rows)] * 2 + totals
        ),
        in_specs=in_vmem(7) + [anywhere] * 8,
        out_specs=tuple(in_vmem(2) + [anywhere] * 6),
        scratch_shapes=[
            vmem(w_query.shape), vmem(w_key_t.shape), vmem(w_value_t.shape), vmem(w_out.shape),
            vmem(w_gate.shape), vmem(w_up.shape), vmem(w_down_t.shape), vmem((features, rows)),
            vmem((levels, ID_ROWS + 2 * KV_HEADS * HEAD_DIM, span)),
            vmem(head_t), vmem(padded), vmem(head_t), vmem(padded),
            vmem((levels, 1, queries), jnp.int32),
            vmem((features, rows)),
            vmem(head_t, f32),
            vmem((KV_HEADS, HEAD_DIM + 16, queries), f32),
            vmem(row, f32), vmem(row, f32),
            vmem((features, rows)),
            *[vmem((features, rows), f32) for _ in range(3)],
            vmem(head_t, f32),
            vmem((count, span, 2 * HEAD_DIM)),
            vmem((count, rows, 2 * HEAD_DIM)), vmem((count, rows, 2 * HEAD_DIM)),
            vmem((2 * KV_HEADS * HEAD_DIM, rows)), vmem((HEADS * HEAD_DIM, rows)),
            vmem((HEAD_DIM // 2, rows), f32), vmem((HEAD_DIM // 2, rows), f32),
            vmem((rows, features)),
            *[vmem(shape) for shape in totals],
            lands,
            dma(8),
            *[dma(levels, KV_HEADS) for _ in range(4)],
            *[dma(count) for _ in range(4)],
            dma(len(jobs), semaphores), dma(len(jobs), semaphores),
        ],
        compiler_params=pltpu.CompilerParams(
            collective_id=1, has_side_effects=True, vmem_limit_bytes=60 * 1024 * 1024
        ),
        name="layer",
    )(
        x_t, ids, attn_gain, ffn_gain, *rotary_tables(rows), w_query, w_key_t, w_value_t, w_out,
        w_gate, w_up, w_down_t, cotangent_t,
    )


PIECES = 2
SOME_ROWS = 48


def finish_kernel(
    layer_in, input_in, gate, up, down_t, out, query, kv,
    layer_out, input_out, gate_out, up_out, down_out, out_out, key_out, value_out, query_out,
    gain_ffn, gain_attn,
    held, made, out_held, out_made, query_held, query_made, kv_held, key_made, value_made, passed,
    come, go,
):
    features = gate.shape[0]
    piece = features // PIECES
    passed_in = [
        pltpu.make_async_copy(source, passed.at[number], come.at[3 * PIECES + 3 + number])
        for number, source in enumerate((layer_in, input_in))
    ]
    passed_out = [
        pltpu.make_async_copy(passed.at[number], target, go.at[number])
        for number, target in enumerate((layer_out, input_out))
    ]
    wide = []
    for source, target in ((gate, gate_out), (up, up_out), (down_t, down_out)):
        for number in range(PIECES):
            rows, at = pl.ds(number * piece, piece), len(wide)
            wide.append(
                (
                    pltpu.make_async_copy(source.at[rows], held.at[at], come.at[at]),
                    pltpu.make_async_copy(made.at[at], target.at[rows], go.at[2 + at]),
                )
            )
    at = len(wide)
    small_in = [
        pltpu.make_async_copy(source, target, come.at[at + number])
        for number, (source, target) in enumerate(
            ((out, out_held), (query, query_held), (kv, kv_held))
        )
    ]
    small_out = [
        pltpu.make_async_copy(source, target, go.at[2 + at + number])
        for number, (source, target) in enumerate(
            (
                (out_made, out_out), (query_made, query_out), (key_made, key_out),
                (value_made, value_out),
            )
        )
    ]
    for arrival, _ in wide:
        arrival.start()
    for copy in small_in + passed_in:
        copy.start()

    def by_rows(count, convert):
        def some(step, carry):
            convert(pl.ds(pl.multiple_of(step * SOME_ROWS, 16), SOME_ROWS), step * SOME_ROWS)
            return carry

        lax.fori_loop(0, count // SOME_ROWS, some, 0)

    for at, (arrival, departure) in enumerate(wide):
        arrival.wait()

        def convert(rows, start, at=at):
            made[at, rows, :] = held[at, rows, :].astype(jnp.float32)

        by_rows(piece, convert)
        departure.start()

    small_in[0].wait()

    def convert_out(rows, start):
        out_made[rows, :] = out_held[rows, :].astype(jnp.float32)

    by_rows(features, convert_out)
    small_out[0].start()
    gain_ffn[...] = out_held[OUT_ROWS - 16 :, :].astype(jnp.float32)[-1]
    small_in[1].wait()
    width = GROUPS * HEAD_DIM

    def convert_query(rows, start):
        query_made[rows, :] = jnp.concatenate(
            [
                query_held[
                    pl.ds(pl.multiple_of(head * features + start, 16), SOME_ROWS), :
                ].astype(jnp.float32)[:, :width]
                for head in range(KV_HEADS)
            ],
            axis=1,
        )

    by_rows(features, convert_query)
    small_out[1].start()
    last = query_held[(KV_HEADS - 1) * features :, QUERY_COLUMNS - 128 :].astype(jnp.float32)
    gain_attn[...] = last.T[-1]
    small_in[2].wait()
    for head in range(KV_HEADS):
        at = head * HEAD_DIM
        key_made[at : at + HEAD_DIM, :] = kv_held[2 * at : 2 * at + HEAD_DIM, :].astype(jnp.float32)
        value_made[at : at + HEAD_DIM, :] = kv_held[
            2 * at + HEAD_DIM : 2 * at + 2 * HEAD_DIM, :
        ].astype(jnp.float32)
    small_out[2].start()
    small_out[3].start()
    for arrival, departure in zip(passed_in, passed_out):
        arrival.wait()
        departure.start()
    for copy in passed_out + [departure for _, departure in wide] + small_out:
        copy.wait()


def finish(layer_t, input_t, down_t, gate, up, out, query, kv):
    features, wide = gate.shape
    key_width = KV_HEADS * HEAD_DIM
    f32 = jnp.float32
    anywhere = pl.BlockSpec(memory_space=pl.ANY)
    shape = lambda *dims: jax.ShapeDtypeStruct(dims, f32)
    short = jax.ShapeDtypeStruct(layer_t.shape, layer_t.dtype)
    vmem = lambda *dims: pltpu.VMEM(dims, jnp.bfloat16)
    vmem_f32 = lambda *dims: pltpu.VMEM(dims, f32)
    copies = 3 * PIECES
    return pl.pallas_call(
        finish_kernel,
        out_shape=(
            short, short,
            shape(features, wide), shape(features, wide), shape(features, wide),
            shape(features, features), shape(key_width, features), shape(key_width, features),
            shape(features, features), shape(features), shape(features),
        ),
        in_specs=[anywhere] * 8,
        out_specs=tuple([anywhere] * 9 + in_vmem(2)),
        scratch_shapes=[
            vmem(copies, features // PIECES, wide), vmem_f32(copies, features // PIECES, wide),
            vmem(OUT_ROWS, features), vmem_f32(features, features),
            vmem(*query.shape), vmem_f32(features, features),
            vmem(*kv.shape), vmem_f32(key_width, features), vmem_f32(key_width, features),
            vmem(2, *layer_t.shape),
            pltpu.SemaphoreType.DMA((copies + 5,)), pltpu.SemaphoreType.DMA((copies + 6,)),
        ],
        compiler_params=pltpu.CompilerParams(vmem_limit_bytes=60 * 1024 * 1024),
        name="finish",
    )(layer_t, input_t, gate, up, down_t, out, query, kv)


def in_vmem(count):
    return [pl.BlockSpec(memory_space=pltpu.VMEM)] * count


def on_device(
    hidden_in, segment_ids, w_query, w_key, w_value, w_out, w_gate, w_up, w_down, gain_attn,
    gain_ffn, out_grad,
):
    summed = layer(
        hidden_in[0].T, segment_ids, gain_attn, gain_ffn, w_query, w_key.T, w_value.T,
        w_out, w_gate, w_up, w_down.T, out_grad[0].T,
    )
    (
        layer_t, input_t, grad_gate, grad_up, grad_down_t, grad_out, grad_key_t, grad_value_t,
        grad_query, grad_gain_ffn, grad_gain_attn,
    ) = finish(*summed)
    return (
        layer_t.T[None], input_t.T[None], grad_query, grad_key_t.T, grad_value_t.T, grad_out,
        grad_gate, grad_up, grad_down_t.T, grad_gain_attn, grad_gain_ffn,
    )


def solution(mesh):
    rows = P("dp", "ctx", None)
    return jax.shard_map(
        on_device,
        mesh=mesh,
        in_specs=(rows, P("dp", "ctx")) + (P(),) * 9 + (rows,),
        out_specs=(rows, rows) + (P(),) * 9,
        check_vma=False,
    )
```

time: 1100 us -> 147 us (0.13); the launches traced: 1080 us -> 147 us
  local copies, waits for them, and re-layouts: 347 us -> 0 us
  waiting for transfers between devices: 274 us -> 0 us
  matrix products: 207 us -> 0 us
  Pallas kernels: 0 us -> 146 us
  other arithmetic: 146 us -> 0 us
  blocking collectives: 59.1 us -> 0 us
  loops' own time: 29.9 us -> 0 us
  between operations: 14.2 us -> 0.84 us
    psum x1 -> x0, waiting for transfers between devices: 210 us -> none  [on_device(): lax.psum((grad_query, grad_key, grad_value, grad_out, grad_gate, grad_up,...]
    dot_general x153 -> x0, matrix products: 207 us -> none  [the longest x24 32.2 us: grad_block(): jnp.einsum('qhgd,khd->hgqk', query_rows, key_block, preferred_element_typ...]
    dynamic_update_slice x48 -> x0, local copies, waits for them, and re-layouts: 179 us -> none  [turn_body(): lax.scan(grad_block, query_grad, (key_span, value_span, local_offsets))]
    pallas_call x0 -> x2, Pallas kernels: none -> 146 us  [the longest x1 138 us: layer(): pl.pallas_call(functools.partial(layer_kernel, order, level_bits, jobs, p...]
    convert_element_type x37 -> x0, other arithmetic: 55.8 us -> none  [the longest x8 14.2 us: turn_body(): key_grad.astype(jnp.bfloat16)]
    dynamic_slice x68 -> x0, local copies, waits for them, and re-layouts: 49.1 us -> none  [the longest x24 14 us: turn_body(): lax.scan(grad_block, query_grad, (key_span, value_span, local_offsets))]
    psum x1 -> x0, blocking collectives: 44.8 us -> none  [on_device(): lax.psum((grad_query, grad_key, grad_value, grad_out, grad_gate, grad_up,...]
    all_gather x2 -> x0, waiting for transfers between devices: 35.7 us -> none  [the longest x1 18.3 us: on_device(): value_piece = lax.all_gather(value_rows, 'ctx', axis=0, tiled=True)]
  transfers between devices with their start and end apart: 19 -> 0, of which waited for: 19 -> 0; matrix products, arithmetic and copies ran while one was open for 4% -> 0% of each run, Pallas kernels for 0% -> 0%
where the time goes in v1:
time: 147 us
  Pallas kernels  146 us (99%)
    pallas_call x1, Pallas kernels, layer(): pl.pallas_call(functools.partial(layer_kernel, order, level_bits, jobs, p...  138 us
    pallas_call x1, Pallas kernels, finish(): pl.pallas_call(finish_kernel, out_shape=(short, short, shape(features, wi...  8.33 us

profile of v1, /device:TPU:1, one launch (start us, length us, event | category | flops | bytes accessed | tf_op | source)
XLA Modules:
  0.0 147.2 jit_solution(18383906146632658164)
XLA Ops:
  0.6 138.0 %layer.1 = (bf16[576,384]{1,0:T(8,128)(2,1)}, bf16[576,384]{1,0:T(8,128)(2,1)}, bf16[576,1536]{1,0:T(8,128)(2,1)}, bf16[576,1536]{1,0:T(8,128)(2,1)}, bf16[576,1...) custom-call(bf16[576,384]{1,0:T(8,128)(2,1)} %bitcast.19, ...), custom_call_target="tpu_custom_call" | custom-call | tf_op jit(solution)/shard_map/layer/pallas_call | solution.py:906
  138.7 8.3 %finish.1 = (bf16[576,384]{1,0:T(8,128)(2,1)}, bf16[576,384]{1,0:T(8,128)(2,1)}, f32[576,1536]{1,0:T(8,128)}, f32[576,1536]{1,0:T(8,128)}, f32[576,1536]{1,0:T(8...) custom-call(bf16[576,384]{1,0:T(8,128)(2,1)} %get-tuple-element.30.l, ...), custom_call_target="tpu_custom_call" | custom-call | tf_op jit(solution)/shard_map/finish/pallas_call | solution.py:1068

commit v2 on v1

--- a/solution.py
+++ b/solution.py
@@ -48,21 +48,34 @@
     return lax.rem(lax.div(place, bit), 2)
 
 
-def flipped(axis, bit):
-    place = lax.axis_index(axis)
-    return {axis: place + (1 - 2 * bit_of(place, bit)) * bit}
-
-
 def plane_order(dp_count):
     bits = [1 << i for i in range(dp_count.bit_length() - 1)]
     return [("ctx", 1, 1)] + [("dp", bit, bits[(i + 1) % len(bits)]) for i, bit in enumerate(bits)]
 
 
-def mirrored(size):
-    place = lax.axis_index("ctx")
+def sum_links(order, level_bits, slice_place, place):
     core, level = lax.rem(place, 2), lax.div(place, 2)
-    group = lax.div(level, size) * size
-    return {"ctx": 2 * (2 * group + size - 1 - level) + core}
+    picks, devices = [], []
+    for axis, first, second in order:
+        at = slice_place if axis == "dp" else place
+        pick, bit = bit_of(at, first), first
+        if second != first:
+            pick = jnp.where(core == 0, pick, bit_of(at, second))
+            bit = jnp.where(core == 0, first, second)
+        partner = at + (1 - 2 * pick) * bit
+        picks.append(pick)
+        devices.append((partner, place) if axis == "dp" else (slice_place, partner))
+    mirrors = []
+    for number in range(level_bits):
+        size = 2 << number
+        group = lax.div(level, size) * size
+        mirrors.append((slice_place, 2 * (2 * group + size - 1 - level) + core))
+    return picks, devices, mirrors
+
+
+def crossed_order(order, ctx_count):
+    bits = [1 << i for i in range(1, ctx_count.bit_length() - 1)]
+    return order + [("ctx", bit, bits[(i + 1) % len(bits)]) for i, bit in enumerate(bits)]
 
 
 def is_inner(level):
@@ -70,6 +83,7 @@
 
 
 HALVINGS = 3
+SLOTS = 5
 
 
 def halved_shapes(rows, columns, cuts):
@@ -82,17 +96,19 @@
 
 def landing_shapes(rows, columns, cuts, plane, level_bits):
     shapes = halved_shapes(rows, columns, cuts)
-    return shapes + [shapes[-1]] * (plane - len(cuts) + level_bits + 1)
+    last = shapes[-1] if shapes else (rows, columns)
+    return shapes + [last] * (plane - len(cuts) + (level_bits + 1 if level_bits else 0))
 
 
 class Summed:
-    def __init__(self, order, level_bits, cuts, source, corner, shape, landed, total, send, recv):
-        self.order, self.level_bits, self.cuts = order, level_bits, cuts
+    def __init__(self, links, level_bits, cuts, source, corner, shape, landed, total, send, recv):
+        self.picks, self.devices, self.mirrors = links
+        self.level_bits, self.cuts = level_bits, cuts
         self.landed, self.total = landed, total
         self.source, self.corner, self.shape = source, corner, shape
         self.send, self.recv = send, recv
-        self.plane = len(order)
-        self.count = self.plane + level_bits + 1
+        self.plane = len(self.picks)
+        self.count = self.plane + (level_bits + 1 if level_bits else 0)
         self.final = landed[-1]
 
     def cut_at(self, corner, shape, cut, pick):
@@ -120,16 +136,6 @@
             return self.source, self.corner, self.shape
         return self.landed[stage - 1], (0, 0), self.landed[stage - 1].shape
 
-    def link(self, stage):
-        axis, first, second = self.order[stage]
-        if first == second:
-            return axis, first
-        return axis, jnp.where(lax.rem(lax.axis_index("ctx"), 2) == 0, first, second)
-
-    def spot(self, stage):
-        axis, bit = self.link(stage)
-        return bit_of(lax.axis_index(axis), bit)
-
     def copy(self, source, target, number, device):
         return pltpu.make_async_remote_copy(
             src_ref=source, dst_ref=target, send_sem=self.send.at[number],
@@ -139,20 +145,21 @@
     def outgoing(self, stage):
         ref, corner, shape = self.current(stage)
         if stage < self.plane:
-            device = flipped(*self.link(stage))
+            device = self.devices[stage]
             if stage < len(self.cuts):
-                corner, shape = self.cut_at(corner, shape, self.cuts[stage], 1 - self.spot(stage))
+                corner, shape = self.cut_at(corner, shape, self.cuts[stage], 1 - self.picks[stage])
         elif stage == self.plane or stage == self.count - 1:
-            device = mirrored(2)
+            device = self.mirrors[0]
         else:
-            device = mirrored(2 << (stage - self.plane))
-        source = self.final if stage == self.count - 1 else self.view(ref, corner, shape)
+            device = self.mirrors[stage - self.plane]
+        given = self.level_bits and stage == self.count - 1
+        source = self.final if given else self.view(ref, corner, shape)
         return self.copy(source, self.landed[stage], stage, device)
 
     def add(self, stage, target=None):
         ref, corner, shape = self.current(stage)
         if stage < len(self.cuts):
-            corner, shape = self.cut_at(corner, shape, self.cuts[stage], self.spot(stage))
+            corner, shape = self.cut_at(corner, shape, self.cuts[stage], self.picks[stage])
         landed = self.landed[stage]
         target = landed if target is None else target
         row, column = corner
@@ -173,7 +180,7 @@
     def share(self, depth):
         corner, shape = (0, 0), self.shape
         for stage in range(depth):
-            corner, shape = self.cut_at(corner, shape, self.cuts[stage], self.spot(stage))
+            corner, shape = self.cut_at(corner, shape, self.cuts[stage], self.picks[stage])
         return self.view(self.total, (corner[0] + self.corner[0], corner[1] + self.corner[1]), shape)
 
     def settle(self):
@@ -185,7 +192,7 @@
         stage = len(self.cuts) - 1 - back
         mine = self.share(stage + 1)
         return self.copy(
-            self.final if back == 0 else mine, mine, self.count + back, flipped(*self.link(stage))
+            self.final if back == 0 else mine, mine, self.count + back, self.devices[stage]
         )
 
     def run(self, op, inner):
@@ -196,6 +203,12 @@
             self.add(op - 1)
             if op < self.plane:
                 self.outgoing(op).start()
+            elif not self.level_bits:
+                self.settle().start()
+                if self.cuts:
+                    self.handing(0).start()
+                else:
+                    self.settle().wait()
             else:
                 @pl.when(jnp.logical_not(inner))
                 def _():
@@ -230,14 +243,15 @@
         for stage in range(self.plane):
             self.outgoing(stage).wait_send()
 
-        @pl.when(inner)
-        def _():
-            for stage in range(self.plane + 1, self.count):
-                self.outgoing(stage).wait_send()
-
-        @pl.when(jnp.logical_not(inner))
-        def _():
-            self.outgoing(self.plane).wait_send()
+        if self.level_bits:
+            @pl.when(inner)
+            def _():
+                for stage in range(self.plane + 1, self.count):
+                    self.outgoing(stage).wait_send()
+
+            @pl.when(jnp.logical_not(inner))
+            def _():
+                self.outgoing(self.plane).wait_send()
 
         for back in range(len(self.cuts)):
             self.handing(back).wait_send()
@@ -253,12 +267,12 @@
 
 def planned(jobs, slots, relayed):
     work = []
-    for plane, level_bits, cuts, size, _ in jobs:
+    for plane, crossed, level_bits, cuts, size, _ in jobs:
         sizes = []
         for stage in range(plane):
             size = size / 2 if stage < len(cuts) else size
             sizes.append(("dp" if stage else "core", size))
-        levels = [("ctx", size)] * (level_bits + 1)
+        levels = [("ctx", size)] * (crossed if crossed else level_bits + 1)
         levels = [(name + str(number), size) for number, (name, size) in enumerate(levels)]
         work.append(sizes + levels + sizes[: len(cuts)][::-1])
     free, arrival, done, plan = {}, {}, [0] * len(jobs), []
@@ -281,7 +295,7 @@
             for link in ("ctx0", "ctx1"):
                 free[link] = max(free.get(link, 0.0), now) + 2.2
         for number, job in enumerate(jobs):
-            if job[4] == slot:
+            if job[5] == slot:
                 plan.append((slot, number, 0))
                 issue(number, now)
         for number in sorted((n for n in live() if arrival[n] <= now), key=lambda n: -done[n]):
@@ -348,16 +362,16 @@
 
 
 def layer_kernel(
-    order, level_bits, jobs, pumps, after,
+    order, crossed, level_bits, jobs, pumps, after,
     x_ref, id_ref, attn_gain_ref, ffn_gain_ref, cosine_in, sine_in, inverse_in,
     query_hbm, key_hbm, value_hbm, out_hbm, gate_hbm, up_hbm, down_hbm, cotangent_hbm,
     layer_out, input_grad, down_total, gate_total, up_total, out_total, query_total,
-    kv_total,
+    kv_total, gain_total,
     query_w, key_w, value_w, out_w, gate_w, up_w, down_w, cotangent_ref,
     kv, query_ref, query_pad, grad_ref, grad_pad, first_ref, normed_t, attended, acc, top,
     delta_ref, mixed_t, residual_t, unit_t, normed_grad, back, part, from_mate, from_above, turned_kv,
     turned_query, back_cosine, back_sine, turned_cotangent,
-    down_part, gate_part, up_part, out_part, query_part, kv_part, lands,
+    down_part, gate_part, up_part, out_part, query_part, kv_part, gain_part, lands,
     loads, up_send, below_recv, over_send, over_recv, mate_send, mate_recv, down_send, above_recv,
     sum_send, sum_recv,
 ):
@@ -368,9 +382,14 @@
     features = x_ref.shape[0]
     wide = gate_w.shape[1]
     count = KV_HEADS * levels
-    mate = {"ctx": place + 1 - 2 * core}
-    below = {"ctx": place - 2}
-    above = {"ctx": place + 2}
+    slice_place = lax.axis_index("dp")
+    mate = (slice_place, place + 1 - 2 * core)
+    below = (slice_place, place - 2)
+    above = (slice_place, place + 2)
+    links = {
+        True: sum_links(order, level_bits, slice_place, place),
+        False: sum_links(crossed, 0, slice_place, place),
+    }
     own = pl.ds(pl.multiple_of(core * rows, 128), rows)
 
     weights = [
@@ -389,9 +408,9 @@
     carries = is_inner(level)
     side = 2 * bit_of(level, 1) - 1
     other = level + side
-    certain = [flipped(axis, bit) for axis, bit, _ in order] + [mirrored(2)]
-    perhaps = [({"ctx": place + 2 * side}, (other >= 0) & (other < levels))]
-    perhaps += [(mirrored(2 << bit), carries) for bit in range(2, level_bits)]
+    certain = links[False][1]
+    perhaps = [((slice_place, place + 2 * side), (other >= 0) & (other < levels))]
+    perhaps += [(device, carries) for device in links[True][2][2:]]
     greet(certain, perhaps)
 
     sources = [(down_part, down_total), (gate_part, gate_total), (up_part, up_total)]
@@ -402,12 +421,13 @@
             (query_part, query_total, (head * features, 0)),
             (kv_part, kv_total, (head * 2 * HEAD_DIM, 0)),
         ]
+    places += [(gain_part, gain_total, (0, 0))]
     streams = [
         Summed(
-            order, level_bits, cuts, source, corner, shape, lands[number], total,
+            links[folded], level_bits if folded else 0, cuts, source, corner, shape, lands[number], total,
             sum_send.at[number], sum_recv.at[number],
         )
-        for number, ((source, total, corner), (cuts, shape)) in enumerate(zip(places, jobs))
+        for number, ((source, total, corner), (folded, cuts, shape)) in enumerate(zip(places, jobs))
     ]
 
     def pump(slot):
@@ -768,15 +788,19 @@
             for head in range(KV_HEADS):
                 @pl.when(ended == head)
                 def _(head=head):
-                    if head < KV_HEADS - 1:
-                        streams[3 * chunks + 1 + 2 * head].run(0, carries)
+                    streams[3 * chunks + 1 + 2 * head].run(0, carries)
                     streams[3 * chunks + 2 + 2 * head].run(0, carries)
 
-        for slot in sorted(pumps):
-            if slot > chunks:
-                @pl.when(turn_number == slot - chunks - 1)
-                def _(slot=slot):
-                    pump(slot)
+        for begin in range(0, 2 * (count + 1), SLOTS):
+            some = range(begin, begin + SLOTS)
+
+            @pl.when((turn_number >= begin) & (turn_number < begin + SLOTS))
+            def _(some=some):
+                for number in some:
+                    if number + chunks + 1 in pumps:
+                        @pl.when(turn_number == number)
+                        def _(slot=number + chunks + 1):
+                            pump(slot)
 
         return carry
 
@@ -794,17 +818,16 @@
     inverse_attn = lax.rsqrt(mean + NORM_EPS)
     unit = x * inverse_attn
     gain_column = jnp.sum(grad_t * unit, axis=1, keepdims=True)
-    last_rows = slice((KV_HEADS - 1) * features, KV_HEADS * features)
-    last = query_part[last_rows, QUERY_COLUMNS - 128 :].astype(jnp.float32)
-    spare = lax.broadcasted_iota(jnp.int32, last.shape, 1) >= HEAD_DIM
-    query_part[last_rows, QUERY_COLUMNS - 128 :] = jnp.where(spare, gain_column, last).astype(
-        jnp.bfloat16
-    )
-    streams[3 * chunks + 2 * KV_HEADS - 1].run(0, carries)
+    gain_rows = jnp.broadcast_to(gain_column, (features, 128)).T
+    gain_part[...] = gain_rows[: gain_part.shape[0]].astype(jnp.bfloat16)
+    streams[-1].run(0, carries)
+    first_ops = len(after) // 3
+    for number, op in after[:first_ops]:
+        streams[number].run(op, carries)
     inner = grad_t * as_column(attn_gain_ref[...].reshape(1, features))
     mean = jnp.sum(inner * unit, axis=0, keepdims=True) * (1.0 / features)
     input_grad[...] = (residual_t[...] + inverse_attn * (inner - unit * mean)).astype(jnp.bfloat16)
-    for number, op in after:
+    for number, op in after[first_ops:]:
         streams[number].run(op, carries)
     for stream in streams:
         stream.drain(carries)
@@ -852,6 +875,7 @@
           w_down_t, cotangent_t):
     dp_count, ctx_count = lax.axis_size("dp"), lax.axis_size("ctx")
     order = plane_order(dp_count)
+    crossed = crossed_order(order, ctx_count)
     level_bits = (ctx_count // 2).bit_length() - 1
     levels = ctx_count // 2
     features, rows = x_t.shape
@@ -860,8 +884,12 @@
     count = KV_HEADS * levels
     chunks = wide // FF_CHUNK
 
-    heads = [("rrc", (features, QUERY_COLUMNS)), ("rrr", (2 * HEAD_DIM, features))] * KV_HEADS
-    jobs = [("rrc", (features, FF_CHUNK))] * (3 * chunks) + [("rrr", (OUT_ROWS, features))] + heads
+    jobs = [(True, "rrc", (features, FF_CHUNK))] * (3 * chunks)
+    jobs += [(True, "rrr", (OUT_ROWS, features))]
+    for head in range(KV_HEADS):
+        folded = head < KV_HEADS - 1
+        jobs += [(folded, "rrc", (features, QUERY_COLUMNS)), (folded, "rrr", (2 * HEAD_DIM, features))]
+    jobs += [(False, "", (16, features))]
     slots = [FEED_US * number for number in range(chunks)]
     slots.append(slots[-1] + OUT_US)
     turns = 2 * (count + 1)
@@ -870,15 +898,18 @@
     begins = [number // 3 for number in range(3 * chunks)] + [chunks]
     for head in range(KV_HEADS):
         begins += [chunks + 2 * (head + 1) * levels + 2] * 2
-    begins[-2] = len(slots) - 1
+    begins += [len(slots) - 1]
     relayed = [
         chunks + 2 + 2 * step for step in range(count) if step % levels < levels - 1
     ]
     pumps, after = {}, []
     for slot, number, op in planned(
         [
-            (len(order), level_bits, cuts, 2 * shape[0] * shape[1], begin)
-            for (cuts, shape), begin in zip(jobs, begins)
+            (
+                len(order), 0 if folded else level_bits, level_bits, cuts, 2 * shape[0] * shape[1],
+                begin,
+            )
+            for (folded, cuts, shape), begin in zip(jobs, begins)
         ],
         slots, relayed,
     ):
@@ -891,8 +922,15 @@
 
     vmem = lambda shape, dtype=jnp.bfloat16: pltpu.VMEM(shape, dtype)
     lands = [
-        [vmem(size) for size in landing_shapes(*shape, cuts, len(order), level_bits)]
-        for cuts, shape in jobs
+        [
+            vmem(size)
+            for size in (
+                landing_shapes(*shape, cuts, len(order), level_bits)
+                if folded
+                else landing_shapes(*shape, cuts, len(crossed), 0)
+            )
+        ]
+        for folded, cuts, shape in jobs
     ]
     dma = lambda *shape: pltpu.SemaphoreType.DMA(shape)
     semaphores = len(order) + level_bits + HALVINGS + 2
@@ -902,14 +940,15 @@
     f32 = jnp.float32
     totals = [(features, wide)] * 3 + [(OUT_ROWS, features)]
     totals += [(KV_HEADS * features, QUERY_COLUMNS), (2 * KV_HEADS * HEAD_DIM, features)]
+    totals += [(16, features)]
     anywhere = pl.BlockSpec(memory_space=pl.ANY)
     return pl.pallas_call(
-        functools.partial(layer_kernel, order, level_bits, jobs, pumps, after),
+        functools.partial(layer_kernel, order, crossed, level_bits, jobs, pumps, after),
         out_shape=tuple(
             jax.ShapeDtypeStruct(shape, jnp.bfloat16) for shape in [(features, rows)] * 2 + totals
         ),
         in_specs=in_vmem(7) + [anywhere] * 8,
-        out_specs=tuple(in_vmem(2) + [anywhere] * 6),
+        out_specs=tuple(in_vmem(2) + [anywhere] * 7),
         scratch_shapes=[
             vmem(w_query.shape), vmem(w_key_t.shape), vmem(w_value_t.shape), vmem(w_out.shape),
             vmem(w_gate.shape), vmem(w_up.shape), vmem(w_down_t.shape), vmem((features, rows)),
@@ -950,7 +989,7 @@
 
 
 def finish_kernel(
-    layer_in, input_in, gate, up, down_t, out, query, kv,
+    layer_in, input_in, gate, up, down_t, out, query, kv, gain,
     layer_out, input_out, gate_out, up_out, down_out, out_out, key_out, value_out, query_out,
     gain_ffn, gain_attn,
     held, made, out_held, out_made, query_held, query_made, kv_held, key_made, value_made, passed,
@@ -1037,8 +1076,7 @@
 
     by_rows(features, convert_query)
     small_out[1].start()
-    last = query_held[(KV_HEADS - 1) * features :, QUERY_COLUMNS - 128 :].astype(jnp.float32)
-    gain_attn[...] = last.T[-1]
+    gain_attn[...] = gain[...].astype(jnp.float32)[-1]
     small_in[2].wait()
     for head in range(KV_HEADS):
         at = head * HEAD_DIM
@@ -1055,7 +1093,7 @@
         copy.wait()
 
 
-def finish(layer_t, input_t, down_t, gate, up, out, query, kv):
+def finish(layer_t, input_t, down_t, gate, up, out, query, kv, gain):
     features, wide = gate.shape
     key_width = KV_HEADS * HEAD_DIM
     f32 = jnp.float32
@@ -1073,7 +1111,7 @@
             shape(features, features), shape(key_width, features), shape(key_width, features),
             shape(features, features), shape(features), shape(features),
         ),
-        in_specs=[anywhere] * 8,
+        in_specs=[anywhere] * 8 + in_vmem(1),
         out_specs=tuple([anywhere] * 9 + in_vmem(2)),
         scratch_shapes=[
             vmem(copies, features // PIECES, wide), vmem_f32(copies, features // PIECES, wide),
@@ -1085,7 +1123,7 @@
         ],
         compiler_params=pltpu.CompilerParams(vmem_limit_bytes=60 * 1024 * 1024),
         name="finish",
-    )(layer_t, input_t, gate, up, down_t, out, query, kv)
+    )(layer_t, input_t, gate, up, down_t, out, query, kv, gain)
 
 
 def in_vmem(count):

time: 147 us -> 146 us (level)
    pallas_call x1, Pallas kernels: 138 us -> 136 us  [layer(): pl.pallas_call(functools.partial(layer_kernel, order, crossed, level_bits...]
where the time goes in v2:
time: 146 us
  Pallas kernels  145 us (99%)
    pallas_call x1, Pallas kernels, layer(): pl.pallas_call(functools.partial(layer_kernel, order, crossed, level_bits...  136 us
    pallas_call x1, Pallas kernels, finish(): pl.pallas_call(finish_kernel, out_shape=(short, short, shape(features, wi...  9.05 us

profile of v2, /device:TPU:1, one launch (start us, length us, event | category | flops | bytes accessed | tf_op | source)
XLA Modules:
  0.0 145.6 jit_solution(14409562109279745845)
XLA Ops:
  0.6 135.7 %layer.1 = (bf16[576,384]{1,0:T(8,128)(2,1)}, bf16[576,384]{1,0:T(8,128)(2,1)}, bf16[576,1536]{1,0:T(8,128)(2,1)}, bf16[576,1536]{1,0:T(8,128)(2,1)}, bf16[576,1...) custom-call(bf16[576,384]{1,0:T(8,128)(2,1)} %bitcast.19, ...), custom_call_target="tpu_custom_call" | custom-call | tf_op jit(solution)/shard_map/layer/pallas_call | solution.py:945
  136.3 9.1 %finish.1 = (bf16[576,384]{1,0:T(8,128)(2,1)}, bf16[576,384]{1,0:T(8,128)(2,1)}, f32[576,1536]{1,0:T(8,128)}, f32[576,1536]{1,0:T(8,128)}, f32[576,1536]{1,0:T(8...) custom-call(bf16[576,384]{1,0:T(8,128)(2,1)} %get-tuple-element.31.l, ...), custom_call_target="tpu_custom_call" | custom-call | tf_op jit(solution)/shard_map/finish/pallas_call | solution.py:1106

commit v3 on v2

--- a/solution.py
+++ b/solution.py
@@ -337,11 +337,11 @@
 
 
 def first_allowed(kv_ref, chip, id_row):
-    return before(kv_ref[chip, pl.ds(0, ID_ROWS), :], id_row)
-
-
-def first_in_half(kv_ref, chip, columns, id_row):
-    return before(kv_ref[chip, pl.ds(0, ID_ROWS), columns], id_row)
+    return sum(before(kv_ref[chip, core, pl.ds(0, ID_ROWS), :], id_row) for core in (0, 1))
+
+
+def first_in_half(kv_ref, chip, core, id_row):
+    return before(kv_ref[chip, core, pl.ds(0, ID_ROWS), :], id_row)
 
 
 def turn(values, cosine, sine_table):
@@ -355,6 +355,20 @@
         ],
         axis=0,
     )
+
+
+def stack_halves(ref, at, values):
+    rows, columns = values.shape
+    values = values.astype(jnp.bfloat16)
+    if not isinstance(at, int):
+        at = pl.multiple_of(at, 16)
+    ref[pl.ds(at, rows), :] = values[:, : columns // 2]
+    ref[pl.ds(at + rows, rows), :] = values[:, columns // 2 :]
+
+
+def with_lanes(values, lanes):
+    fill = jnp.zeros((values.shape[0], lanes - values.shape[1]), values.dtype)
+    return jnp.concatenate([values, fill], axis=1)
 
 
 def as_column(row):
@@ -377,10 +391,11 @@
 ):
     place = lax.axis_index("ctx")
     core, level = lax.rem(place, 2), lax.div(place, 2)
-    levels, _, span = kv.shape
-    rows = span // 2
+    levels, _, _, rows = kv.shape
+    span = 2 * rows
     features = x_ref.shape[0]
     wide = gate_w.shape[1]
+    chunks = wide // FF_CHUNK
     count = KV_HEADS * levels
     slice_place = lax.axis_index("dp")
     mate = (slice_place, place + 1 - 2 * core)
@@ -414,11 +429,13 @@
     greet(certain, perhaps)
 
     sources = [(down_part, down_total), (gate_part, gate_total), (up_part, up_total)]
-    places = [(*pair, (0, at)) for at in range(0, wide, FF_CHUNK) for pair in sources]
+    places = [
+        (*pair, (2 * features * number, 0)) for number in range(wide // FF_CHUNK) for pair in sources
+    ]
     places += [(out_part, out_total, (0, 0))]
     for head in range(KV_HEADS):
         places += [
-            (query_part, query_total, (head * features, 0)),
+            (query_part, query_total, (2 * head * features, 0)),
             (kv_part, kv_total, (head * 2 * HEAD_DIM, 0)),
         ]
     places += [(gain_part, gain_total, (0, 0))]
@@ -443,7 +460,7 @@
     base_cosine, base_sine = jnp.cos(base), jnp.sin(base)
     cosine = base_cosine * cosine_in[...] - base_sine * sine_in[...]
     sine_table = base_sine * cosine_in[...] + base_cosine * sine_in[...]
-    kv[level, pl.ds(0, ID_ROWS), own] = jnp.broadcast_to(
+    kv[level, core, pl.ds(0, ID_ROWS), :] = jnp.broadcast_to(
         id_ref[...].astype(jnp.float32), (ID_ROWS, rows)
     ).astype(jnp.bfloat16)
     weights[0].wait()
@@ -456,14 +473,14 @@
 
     def upward(chip, head):
         return pltpu.make_async_remote_copy(
-            src_ref=kv.at[chip, piece_rows(head), own], dst_ref=kv.at[chip, piece_rows(head), own],
+            src_ref=kv.at[chip, core, piece_rows(head)], dst_ref=kv.at[chip, core, piece_rows(head)],
             send_sem=up_send.at[chip, head], recv_sem=below_recv.at[chip, head],
             device_id=above, device_id_type=MESH,
         )
 
     def across(chip, head):
         return pltpu.make_async_remote_copy(
-            src_ref=kv.at[chip, piece_rows(head), own], dst_ref=kv.at[chip, piece_rows(head), own],
+            src_ref=kv.at[chip, core, piece_rows(head)], dst_ref=kv.at[chip, core, piece_rows(head)],
             send_sem=over_send.at[chip, head], recv_sem=over_recv.at[chip, head],
             device_id=mate, device_id_type=MESH,
         )
@@ -482,7 +499,7 @@
         at = head * HEAD_DIM
         key = turn(keys[at : at + HEAD_DIM], cosine, sine_table)
         both = jnp.concatenate([key, values[at : at + HEAD_DIM]], axis=0)
-        kv[level, pl.ds(ID_ROWS + 2 * at, 2 * HEAD_DIM), own] = both.astype(jnp.bfloat16)
+        kv[level, core, pl.ds(ID_ROWS + 2 * at, 2 * HEAD_DIM), :] = both.astype(jnp.bfloat16)
         hand_on(level, head)
     weights[2].wait()
     queries = transposed_times(query_w[...], normed_t[...])
@@ -510,14 +527,13 @@
 
     def attend_block(chip, half, careful):
         begin = half * rows
-        columns = pl.ds(pl.multiple_of(begin, 128), rows)
         first = first_ref[chip] - begin
         limit = index - chip * span - begin
         inside = first <= 0
         for head in range(KV_HEADS):
             key_at = ID_ROWS + 2 * HEAD_DIM * head
-            key_t = kv[chip, pl.ds(key_at, HEAD_DIM), columns]
-            value_t = kv[chip, pl.ds(key_at + HEAD_DIM, HEAD_DIM), columns]
+            key_t = kv[chip, half, pl.ds(key_at, HEAD_DIM), :]
+            value_t = kv[chip, half, pl.ds(key_at + HEAD_DIM, HEAD_DIM), :]
             scores = transposed_times(key_t, query_ref[head])
             old = top[head]
             if careful:
@@ -558,7 +574,7 @@
 
             @pl.when(mates == 0)
             def _():
-                first_ref[chip] = first_in_half(kv, chip, own, id_row) + half * rows
+                first_ref[chip] = first_in_half(kv, chip, core, id_row) + half * rows
 
             edge = (block == 0) | (block == place)
 
@@ -603,16 +619,17 @@
         sigmoid = 1.0 / (1.0 + jnp.exp(-gate))
         silu = gate * sigmoid
         hidden = (silu * up).astype(jnp.bfloat16)
-        down_part[:, piece] = matmul(cotangent_t, hidden).astype(jnp.bfloat16)
+        at_row = 2 * features * number
+        stack_halves(down_part, at_row, matmul(cotangent_t, hidden))
         streams[3 * number].run(0, carries)
         grad_hidden = matmul(cotangent, down_w[:, piece])
         gate_grad = (grad_hidden * up * sigmoid * (1.0 + gate * (1.0 - sigmoid))).astype(
             jnp.bfloat16
         )
         up_grad = (grad_hidden * silu).astype(jnp.bfloat16)
-        gate_part[:, piece] = matmul(normed_ffn_t, gate_grad).astype(jnp.bfloat16)
+        stack_halves(gate_part, at_row, matmul(normed_ffn_t, gate_grad))
         streams[3 * number + 1].run(0, carries)
-        up_part[:, piece] = matmul(normed_ffn_t, up_grad).astype(jnp.bfloat16)
+        stack_halves(up_part, at_row, matmul(normed_ffn_t, up_grad))
         streams[3 * number + 2].run(0, carries)
         residual_t[...] += times_transposed(down_w[:, piece], hidden)
         normed_grad[...] += times_transposed(gate_w[:, piece], gate_grad) + times_transposed(
@@ -630,9 +647,9 @@
     branch = branch.astype(jnp.bfloat16)
     out_grads = times_transposed(mixed_t[...], branch)
     fill = jnp.broadcast_to(gain_grad, (features, out_part.shape[0] - features)).T
-    out_part[:features, :] = out_grads.astype(jnp.bfloat16)
-    out_part[features:, :] = fill.astype(jnp.bfloat16)
-    chunks = wide // FF_CHUNK
+    lanes = out_part.shape[1]
+    out_part[:features, :] = with_lanes(out_grads, lanes).astype(jnp.bfloat16)
+    out_part[features:, :] = with_lanes(fill, lanes).astype(jnp.bfloat16)
     streams[3 * chunks].run(0, carries)
     mixed_grad = matmul(out_w[...], branch).astype(jnp.bfloat16)
     for head in range(KV_HEADS):
@@ -661,9 +678,8 @@
             less = jnp.where(first <= 0, less, -MASKED)
         for at in range(0, rows, BACK_CHUNK):
             size = min(BACK_CHUNK, rows - at)
-            columns = pl.ds(pl.multiple_of(begin + at, 128), size)
-            key_t = kv[chip, pl.ds(key_at, HEAD_DIM), columns]
-            value_t = kv[chip, pl.ds(value_at, HEAD_DIM), columns]
+            key_t = kv[chip, half, pl.ds(key_at, HEAD_DIM), at : at + size]
+            value_t = kv[chip, half, pl.ds(value_at, HEAD_DIM), at : at + size]
             scores = transposed_times(key_t, query_ref[head])
             if careful:
                 key_index = at + lax.broadcasted_iota(jnp.int32, scores.shape, 0)
@@ -726,9 +742,9 @@
         kv_back = jnp.concatenate([key_back, value_back], axis=0)
         at = pl.multiple_of(head * 2 * HEAD_DIM, 2 * HEAD_DIM)
         turned_kv[pl.ds(at, 2 * HEAD_DIM), :] = kv_back
-        kv_part[pl.ds(at, 2 * HEAD_DIM), :] = times_transposed(kv_back, normed_t[...]).astype(
-            jnp.bfloat16
-        )
+        kv_part[pl.ds(at, 2 * HEAD_DIM), :] = with_lanes(
+            times_transposed(kv_back, normed_t[...]), kv_part.shape[1]
+        ).astype(jnp.bfloat16)
         query_back = jnp.concatenate(
             [
                 turn(
@@ -741,10 +757,8 @@
         )
         wide_at = pl.multiple_of(head * GROUPS * HEAD_DIM, HEAD_DIM)
         turned_query[pl.ds(wide_at, GROUPS * HEAD_DIM), :] = query_back
-        spare = jnp.zeros((features, QUERY_COLUMNS - GROUPS * HEAD_DIM), jnp.float32)
-        query_part[pl.ds(pl.multiple_of(head * features, features), features), :] = jnp.concatenate(
-            [times_transposed(normed_t[...], query_back), spare], axis=1
-        ).astype(jnp.bfloat16)
+        query_grads = with_lanes(times_transposed(normed_t[...], query_back), QUERY_COLUMNS)
+        stack_halves(query_part, 2 * head * features, query_grads)
 
     def one_step(turn_number, carry):
         step, own_turn = lax.div(turn_number, 2), lax.rem(turn_number, 2)
@@ -819,7 +833,9 @@
     unit = x * inverse_attn
     gain_column = jnp.sum(grad_t * unit, axis=1, keepdims=True)
     gain_rows = jnp.broadcast_to(gain_column, (features, 128)).T
-    gain_part[...] = gain_rows[: gain_part.shape[0]].astype(jnp.bfloat16)
+    gain_part[...] = with_lanes(gain_rows[: gain_part.shape[0]], gain_part.shape[1]).astype(
+        jnp.bfloat16
+    )
     streams[-1].run(0, carries)
     first_ops = len(after) // 3
     for number, op in after[:first_ops]:
@@ -884,12 +900,15 @@
     count = KV_HEADS * levels
     chunks = wide // FF_CHUNK
 
-    jobs = [(True, "rrc", (features, FF_CHUNK))] * (3 * chunks)
-    jobs += [(True, "rrr", (OUT_ROWS, features))]
+    jobs = [(True, "rrr", (2 * features, FF_CHUNK // 2))] * (3 * chunks)
+    jobs += [(True, "rrr", (OUT_ROWS, OUT_ROWS))]
     for head in range(KV_HEADS):
         folded = head < KV_HEADS - 1
-        jobs += [(folded, "rrc", (features, QUERY_COLUMNS)), (folded, "rrr", (2 * HEAD_DIM, features))]
-    jobs += [(False, "", (16, features))]
+        jobs += [
+            (folded, "rrr", (2 * features, QUERY_COLUMNS // 2)),
+            (folded, "rrr", (2 * HEAD_DIM, OUT_ROWS)),
+        ]
+    jobs += [(False, "", (16, OUT_ROWS))]
     slots = [FEED_US * number for number in range(chunks)]
     slots.append(slots[-1] + OUT_US)
     turns = 2 * (count + 1)
@@ -938,9 +957,9 @@
     padded = (KV_HEADS, queries, 2 * HEAD_DIM)
     row = (KV_HEADS, 1, queries)
     f32 = jnp.float32
-    totals = [(features, wide)] * 3 + [(OUT_ROWS, features)]
-    totals += [(KV_HEADS * features, QUERY_COLUMNS), (2 * KV_HEADS * HEAD_DIM, features)]
-    totals += [(16, features)]
+    totals = [(2 * features * chunks, FF_CHUNK // 2)] * 3 + [(OUT_ROWS, OUT_ROWS)]
+    totals += [(2 * KV_HEADS * features, QUERY_COLUMNS // 2), (2 * KV_HEADS * HEAD_DIM, OUT_ROWS)]
+    totals += [(16, OUT_ROWS)]
     anywhere = pl.BlockSpec(memory_space=pl.ANY)
     return pl.pallas_call(
         functools.partial(layer_kernel, order, crossed, level_bits, jobs, pumps, after),
@@ -952,7 +971,7 @@
         scratch_shapes=[
             vmem(w_query.shape), vmem(w_key_t.shape), vmem(w_value_t.shape), vmem(w_out.shape),
             vmem(w_gate.shape), vmem(w_up.shape), vmem(w_down_t.shape), vmem((features, rows)),
-            vmem((levels, ID_ROWS + 2 * KV_HEADS * HEAD_DIM, span)),
+            vmem((levels, 2, ID_ROWS + 2 * KV_HEADS * HEAD_DIM, rows)),
             vmem(head_t), vmem(padded), vmem(head_t), vmem(padded),
             vmem((levels, 1, queries), jnp.int32),
             vmem((features, rows)),
@@ -995,8 +1014,9 @@
     held, made, out_held, out_made, query_held, query_made, kv_held, key_made, value_made, passed,
     come, go,
 ):
-    features = gate.shape[0]
+    features, wide_columns = gate_out.shape
     piece = features // PIECES
+    stacked = wide_columns // gate.shape[1]
     passed_in = [
         pltpu.make_async_copy(source, passed.at[number], come.at[3 * PIECES + 3 + number])
         for number, source in enumerate((layer_in, input_in))
@@ -1006,16 +1026,20 @@
         for number, target in enumerate((layer_out, input_out))
     ]
     wide = []
-    for source, target in ((gate, gate_out), (up, up_out), (down_t, down_out)):
-        for number in range(PIECES):
-            rows, at = pl.ds(number * piece, piece), len(wide)
-            wide.append(
-                (
-                    pltpu.make_async_copy(source.at[rows], held.at[at], come.at[at]),
-                    pltpu.make_async_copy(made.at[at], target.at[rows], go.at[2 + at]),
+    for number, (source, target) in enumerate(
+        ((gate, gate_out), (up, up_out), (down_t, down_out))
+    ):
+        arrival = pltpu.make_async_copy(source, held.at[number], come.at[number])
+        departures = []
+        for at in range(PIECES):
+            rows = pl.ds(at * piece, piece)
+            departures.append(
+                pltpu.make_async_copy(
+                    made.at[number, rows], target.at[rows], go.at[2 + number * PIECES + at]
                 )
             )
-    at = len(wide)
+        wide.append((arrival, departures))
+    at = 3 * PIECES
     small_in = [
         pltpu.make_async_copy(source, target, come.at[at + number])
         for number, (source, target) in enumerate(
@@ -1043,58 +1067,68 @@
 
         lax.fori_loop(0, count // SOME_ROWS, some, 0)
 
-    for at, (arrival, departure) in enumerate(wide):
+    for number, (arrival, departures) in enumerate(wide):
         arrival.wait()
-
-        def convert(rows, start, at=at):
-            made[at, rows, :] = held[at, rows, :].astype(jnp.float32)
-
-        by_rows(piece, convert)
-        departure.start()
+        for at in range(PIECES):
+
+            def convert(rows, start, number=number, skip=at * piece):
+                made[
+                    number, pl.ds(pl.multiple_of(skip + start, 16), SOME_ROWS), :
+                ] = jnp.concatenate(
+                    [
+                        held[
+                            number,
+                            pl.ds(pl.multiple_of(column * features + skip + start, 16), SOME_ROWS),
+                            :,
+                        ].astype(jnp.float32)
+                        for column in range(stacked)
+                    ],
+                    axis=1,
+                )
+
+            by_rows(piece, convert)
+            departures[at].start()
 
     small_in[0].wait()
 
     def convert_out(rows, start):
-        out_made[rows, :] = out_held[rows, :].astype(jnp.float32)
+        out_made[rows, :] = out_held[rows, :].astype(jnp.float32)[:, :features]
 
     by_rows(features, convert_out)
     small_out[0].start()
-    gain_ffn[...] = out_held[OUT_ROWS - 16 :, :].astype(jnp.float32)[-1]
+    gain_ffn[...] = out_held[OUT_ROWS - 16 :, :].astype(jnp.float32)[-1:, :features].reshape(features)
     small_in[1].wait()
     width = GROUPS * HEAD_DIM
 
     def convert_query(rows, start):
-        query_made[rows, :] = jnp.concatenate(
-            [
-                query_held[
-                    pl.ds(pl.multiple_of(head * features + start, 16), SOME_ROWS), :
-                ].astype(jnp.float32)[:, :width]
-                for head in range(KV_HEADS)
-            ],
-            axis=1,
-        )
+        pieces = []
+        for number in range(2 * KV_HEADS):
+            at = pl.multiple_of(number * features + start, 16)
+            values = query_held[pl.ds(at, SOME_ROWS), :].astype(jnp.float32)
+            pieces.append(values[:, : width - values.shape[1]] if number % 2 else values)
+        query_made[rows, :] = jnp.concatenate(pieces, axis=1)
 
     by_rows(features, convert_query)
     small_out[1].start()
-    gain_attn[...] = gain[...].astype(jnp.float32)[-1]
+    gain_attn[...] = gain[...].astype(jnp.float32)[-1:, :features].reshape(features)
     small_in[2].wait()
     for head in range(KV_HEADS):
         at = head * HEAD_DIM
-        key_made[at : at + HEAD_DIM, :] = kv_held[2 * at : 2 * at + HEAD_DIM, :].astype(jnp.float32)
-        value_made[at : at + HEAD_DIM, :] = kv_held[
-            2 * at + HEAD_DIM : 2 * at + 2 * HEAD_DIM, :
-        ].astype(jnp.float32)
+        both = kv_held[2 * at : 2 * at + 2 * HEAD_DIM, :].astype(jnp.float32)[:, :features]
+        key_made[at : at + HEAD_DIM, :] = both[:HEAD_DIM]
+        value_made[at : at + HEAD_DIM, :] = both[HEAD_DIM:]
     small_out[2].start()
     small_out[3].start()
     for arrival, departure in zip(passed_in, passed_out):
         arrival.wait()
         departure.start()
-    for copy in passed_out + [departure for _, departure in wide] + small_out:
+    for copy in passed_out + [copy for _, copies in wide for copy in copies] + small_out:
         copy.wait()
 
 
 def finish(layer_t, input_t, down_t, gate, up, out, query, kv, gain):
-    features, wide = gate.shape
+    features = layer_t.shape[0]
+    wide = gate.shape[0] * gate.shape[1] // features
     key_width = KV_HEADS * HEAD_DIM
     f32 = jnp.float32
     anywhere = pl.BlockSpec(memory_space=pl.ANY)
@@ -1114,8 +1148,8 @@
         in_specs=[anywhere] * 8 + in_vmem(1),
         out_specs=tuple([anywhere] * 9 + in_vmem(2)),
         scratch_shapes=[
-            vmem(copies, features // PIECES, wide), vmem_f32(copies, features // PIECES, wide),
-            vmem(OUT_ROWS, features), vmem_f32(features, features),
+            vmem(3, *gate.shape), vmem_f32(3, features, wide),
+            vmem(*out.shape), vmem_f32(features, features),
             vmem(*query.shape), vmem_f32(features, features),
             vmem(*kv.shape), vmem_f32(key_width, features), vmem_f32(key_width, features),
             vmem(2, *layer_t.shape),

time: 146 us -> 146 us (level)
  no operation moved by 1% of the time
where the time goes in v3:
time: 146 us
  Pallas kernels  145 us (99%)
    pallas_call x1, Pallas kernels, layer(): pl.pallas_call(functools.partial(layer_kernel, order, crossed, level_bits...  136 us
    pallas_call x1, Pallas kernels, finish(): pl.pallas_call(finish_kernel, out_shape=(short, short, shape(features, wi...  8.98 us

profile of v3, /device:TPU:1, one launch (start us, length us, event | category | flops | bytes accessed | tf_op | source)
XLA Modules:
  0.0 146.2 jit_solution(2512692943459507195)
XLA Ops:
  0.6 136.3 %layer.1 = (bf16[576,384]{1,0:T(8,128)(2,1)}, bf16[576,384]{1,0:T(8,128)(2,1)}, bf16[3456,256]{1,0:T(8,128)(2,1)}, bf16[3456,256]{1,0:T(8,128)(2,1)}, bf16[3456,...) custom-call(bf16[576,384]{1,0:T(8,128)(2,1)} %bitcast.19, ...), custom_call_target="tpu_custom_call" | custom-call | tf_op jit(solution)/shard_map/layer/pallas_call | solution.py:964
  137.0 9.0 %finish.1 = (bf16[576,384]{1,0:T(8,128)(2,1)}, bf16[576,384]{1,0:T(8,128)(2,1)}, f32[576,1536]{1,0:T(8,128)}, f32[576,1536]{1,0:T(8,128)}, f32[576,1536]{1,0:T(8...) custom-call(bf16[576,384]{1,0:T(8,128)(2,1)} %get-tuple-element.31.l, ...), custom_call_target="tpu_custom_call" | custom-call | tf_op jit(solution)/shard_map/finish/pallas_call | solution.py:1140
